TPU v7x, 128 devices: a whole 4x4x4 slice. The times are simulated.
128 devices in a mesh: dp: 4 (over y_hi, core), mp: 32 (over y_lo, z, x).
Axes of the slice: x: 4, y: 4 (y_hi: 2, y_lo: 2; y = y_hi * 2 + y_lo), z: 4, core: 2. Of those that a mesh axis runs over, the one named last changes fastest.
Arguments:
- gradients: bfloat16 [4, 6, 6144, 1408], P('dp', None, 'mp'), may hold values from -500 to 500
- errors: float32 [4, 6, 6144, 1408], P('dp', None, 'mp'), may hold values from -3 to 3
- previous_q: float32 [6, 64, 1408], replicated, may hold values from -1 to 1, as said below
Outputs:
- new_errors: float32 [4, 6, 6144, 1408], P('dp', None, 'mp')
- new_q: float32 [6, 64, 1408], replicated
Inputs may be any that keep to these rules, and one draw needn't show every extreme that they name: `previous_q`: entries of the previous Q factors, within 5 / sqrt(1408).
All inputs are finite; a program needn't handle non-finite values.
Results may differ from a plain program's by a relative error of at most 0.0003.
Values sent between devices are 32-bit elements; how exact they have to be, the bound alone decides.
A program may use at most 128 MiB of HBM per device.

v0:
```python
import jax
import jax.numpy as jnp
from jax import lax
from jax.sharding import PartitionSpec as P

exact_mode = lax.Precision.HIGHEST


def body(gradients, errors, previous_q):
    replicas = lax.axis_size("dp")
    error_list = []
    factor_list = []
    for which in range(gradients.shape[1]):
        merged = gradients[0, which].astype(jnp.float32) + errors[0, which]
        local_p = lax.dot_general(
            merged, previous_q[which], (((1,), (1,)), ((), ())), precision=exact_mode
        )
        p_mat = lax.psum(local_p, "dp") / replicas
        gram_mat = lax.psum(jnp.dot(p_mat.T, p_mat, precision=exact_mode), "mp")
        factor = jnp.linalg.cholesky(gram_mat)
        ortho = jax.scipy.linalg.solve_triangular(factor, p_mat.T, lower=True).T
        q_terms = lax.dot_general(ortho, merged, (((0,), (0,)), ((), ())), precision=exact_mode)
        q_total = lax.psum(q_terms, ("dp", "mp"))
        q_total = q_total / replicas
        approx = jnp.dot(ortho, q_total, precision=exact_mode)
        error_list.append(merged - approx)
        factor_list.append(q_total)
    new_errors = jnp.stack(error_list, axis=0)[None]
    new_q = jnp.stack(factor_list, axis=0)
    return (new_errors, new_q)


def solution(mesh):
    in_specs = (P("dp", None, "mp", None), P("dp", None, "mp", None), P())
    out_specs = (P("dp", None, "mp", None), P())
    return jax.shard_map(body, mesh=mesh, in_specs=in_specs, out_specs=out_specs, check_vma=False)
```

profile of v0, /device:TPU:1, one launch (start us, length us, event | category | flops | bytes accessed | tf_op | source)
XLA Modules:
  0.0 661.4 jit_solution(12527943925262893056)
XLA Ops:
  7.2 3.5 fusion.14
  10.7 3.5 fusion.18
  14.2 3.2 fusion.22
  17.4 3.1 fusion.26
  20.5 3.1 fusion.30
  23.7 3.1 fusion.34
  26.9 45.9 %all-reduce.11.cloned.1.call-done = (f32[192,64]{0,1:T(8,128)}, f32[192,64]{0,1:T(8,128)}, f32[192,64]{0,1:T(8,128)}, f32[192,64]{0,1:T(8,128)}, f32[192,64]{0,1:T(8,128)}, /*index=5*/f32[192,64]{0,1:T(8,128)}) async-done(((f32[192,64]{0,1:T(8,128)}, f32[192,64]{0,1:T(8,128)}, f32[192,64]{0,1:T(8,128)}, f32[192,64]{0,1:T(8,128)}, f32[192,64]{0,1:T(8,128)}, /*index=5*/f32[192,64]{0,1:T(8,128)}), ...) | async-done | bytes 294928 | tf_op jit(solution)/shard_map/psum | solution.py:18
  81.4 1.7 fusion.88
  83.4 274.9 %all-reduce.9.cloned.1.call-done = (f32[64,64]{0,1:T(8,128)}, f32[64,64]{0,1:T(8,128)}, f32[64,64]{0,1:T(8,128)}, f32[64,64]{0,1:T(8,128)}, f32[64,64]{0,1:T(8,128)}, /*index=5*/f32[64,64]{0,1:T(8,128)}) async-done(((f32[64,64]{0,1:T(8,128)}, f32[64,64]{0,1:T(8,128)}, f32[64,64]{0,1:T(8,128)}, f32[64,64]{0,1:T(8,128)}, f32[64,64]{0,1:T(8,128)}, /*index=5*/f32[64,64]{0,1:T(8,128)}), (f32[64,64]{0,1:T(8,128)}, ...) | async-done | bytes 98320 | tf_op jit(solution)/shard_map/psum | solution.py:19
  360.7 5.8 cholesky.159
  367.9 4.9 custom-call.15
  374.0 2.9 fusion.12
  376.8 5.8 cholesky.148
  384.0 5.5 custom-call.14
  390.6 2.8 fusion.16
  395.7 6.6 cholesky.137
  403.7 4.9 custom-call.13
  408.9 2.9 fusion.20
  411.7 6.6 cholesky.126
  419.7 5.5 custom-call.12
  426.3 2.9 fusion.24
  432.7 6.6 cholesky.115
  441.5 5.7 custom-call.11
  448.3 2.9 fusion.28
  451.1 6.6 cholesky.104
  459.1 4.9 custom-call.10
  465.1 3.1 fusion.32
  468.3 170.2 %all-reduce.7.cloned.1.call-done = (f32[64,1408]{1,0:T(8,128)}, f32[64,1408]{1,0:T(8,128)}, f32[64,1408]{1,0:T(8,128)}, f32[64,1408]{1,0:T(8,128)}, f32[64,1408]{1,0:T(8,128)}, /*index=5*/f32[64,1408]{1,0:T(8,128)}) async-done(((f32[64,1408]{1,0:T(8,128)}, f32[64,1408]{1,0:T(8,128)}, f32[64,1408]{1,0:T(8,128)}, f32[64,1408]{1,0:T(8,128)}, f32[64,1408]{1,0:T(8,128)}, /*index=5*/f32[64,1408]{1,0:T(8,128)}), ...) | async-done | bytes 2162704 | tf_op jit(solution)/shard_map/psum | solution.py:23
  638.5 2.7 fusion.1
  642.4 2.4 fusion.3
  645.9 2.0 fusion.5
  651.4 2.7 copy-done.11
  (87 shorter events, 38.1 us)
Async XLA Ops:
  7.2 7.1 %copy-start = (bf16[1,6,192,1408]{3,2,1,0:T(8,128)(2,1)S(1)}, bf16[1,6,192,1408]{3,2,1,0:T(8,128)(2,1)}, u32[]{:S(2)}) copy-start(bf16[1,6,192,1408]{3,2,1,0:T(8,128)(2,1)} %param.6) | copy-start | bytes 9732100
  7.2 65.6 %all-reduce.11.cloned.1.call-start = ((), (), s32[]{:S(2)}) async-start(), calls=%async_computation.2 | async-start | bytes 786432 | tf_op jit(solution)/shard_map/psum | solution.py:18
  10.7 6.7 %copy-start.2 = (f32[6,64,1408]{2,1,0:T(8,128)S(1)}, f32[6,64,1408]{2,1,0:T(8,128)}, u32[]{:S(2)}) copy-start(f32[6,64,1408]{2,1,0:T(8,128)} %param.8) | copy-start | bytes 6488068
  26.8 331.4 %all-reduce.9.cloned.1.call-start = ((), (), s32[]{:S(2)}) async-start(), calls=%async_computation.1 | async-start | bytes 393216 | tf_op jit(solution)/shard_map/psum | solution.py:19
  72.8 316.8 %copy-start.10 = (f32[192,64]{0,1:T(8,128)S(1)}, f32[192,64]{0,1:T(8,128)}, u32[]{:S(2)}) copy-start(f32[192,64]{0,1:T(8,128)} %get-tuple-element.20) | copy-start | bytes 147460
  83.2 555.3 %all-reduce.7.cloned.1.call-start = ((), (), s32[]{:S(2)}) async-start(), calls=%async_computation | async-start | bytes 4325376 | tf_op jit(solution)/shard_map/psum | solution.py:23
  373.9 19.5 %copy-start.13 = (f32[64,64]{0,1:T(8,128)S(1)}, f32[64,64]{0,1:T(8,128)}, u32[]{:S(2)}) copy-start(f32[64,64]{0,1:T(8,128)} %get-tuple-element.12) | copy-start | bytes 49156
  373.9 34.6 %copy-start.9 = (f32[192,64]{0,1:T(8,128)S(1)}, f32[192,64]{0,1:T(8,128)}, u32[]{:S(2)}) copy-start(f32[192,64]{0,1:T(8,128)} %get-tuple-element.19) | copy-start | bytes 147460
  408.8 20.3 %copy-start.12 = (f32[64,64]{0,1:T(8,128)S(1)}, f32[64,64]{0,1:T(8,128)}, u32[]{:S(2)}) copy-start(f32[64,64]{0,1:T(8,128)} %get-tuple-element.10) | copy-start | bytes 49156
  448.3 2.9 copy-start.7
  465.1 180.8 %slice-start = ((s8[6488064]{0:T(1024)(128)(4,1)}), s8[2293760]{0:T(1024)(128)(4,1)S(1)}, s32[]{:S(2)}) async-start(s8[6488064]{0:T(1024)(128)(4,1)} %bitcast.175), calls=%async_computation.3 | async-start | bytes 4587520
  468.3 174.1 %copy-start.8 = (f32[64,192]{1,0:T(8,128)S(1)}, f32[64,192]{1,0:T(8,128)}, u32[]{:S(2)}) copy-start(f32[64,192]{1,0:T(8,128)} %copy-done.7) | copy-start | bytes 147460
  638.5 3.9 copy-start.1
  638.5 7.4 %slice-start.1 = ((s8[6488064]{0:T(1024)(128)(4,1)}), s8[4194304]{0:T(1024)(128)(4,1)S(1)}, s32[]{:S(2)}) async-start(s8[6488064]{0:T(1024)(128)(4,1)} %bitcast.175), calls=%async_computation.4 | async-start | bytes 8388608
  644.8 3.2 copy-start.6
  644.8 3.2 copy-start.5
  648.0 1.2 copy-start.4
  649.1 1.2 copy-start.3
  651.4 2.8 copy-start.11
  651.4 3.4 copy-start.14
Sparse Core Ops, SparseCore 0:
  27.0 45.7 all-reduce.10
  83.3 274.9 all-reduce.8
  468.4 170.0 all-reduce.6
where the time goes:
time: 663 us; the launch traced here: 661 us
  waiting for transfers between devices  491 us (74%)
  other arithmetic  84.2 us (13%)
  matrix products  63.4 us (10%)
  between operations  14.2 us (2%)
  local copies, waits for them, and re-layouts  8.24 us (1%)
    psum x1, waiting for transfers between devices, body(): gram_mat = lax.psum(jnp.dot(p_mat.T, p_mat, precision=exact_mode), 'mp')  275 us
    psum x1, waiting for transfers between devices, body(): q_total = lax.psum(q_terms, ('dp', 'mp'))  170 us
    psum x1, waiting for transfers between devices, body(): p_mat = lax.psum(local_p, 'dp') / replicas  45.9 us
    another operation x18, other arithmetic, body(): factor = jnp.linalg.cholesky(gram_mat)  42.3 us
    another operation x12, other arithmetic, body(): ortho = jax.scipy.linalg.solve_triangular(factor, p_mat.T, lower=True).T  35.9 us
    dot_general x6, matrix products, body(): lax.dot_general(merged, previous_q[which], (((1,), (1,)), ((), ())), prec...  19.6 us
    dot_general x6, matrix products, body(): lax.dot_general(ortho, merged, (((0,), (0,)), ((), ())), precision=exact_...  17.4 us
  transfers between devices with their start and end apart: 3, of which 3 were waited for; matrix products, arithmetic and copies ran while one was open for 0% of the time, Pallas kernels for 0%

commit v1 on v0

v1 whole, which is shorter than its diff:
```python
import functools

import jax
import jax.numpy as jnp
from jax import lax
from jax.experimental import pallas as pl
from jax.experimental.pallas import tpu as pltpu
from jax.sharding import PartitionSpec as P

MESH = pl.DeviceIdType.MESH
MATS, ROWS, D, R = 6, 192, 1408, 64
HALF = ROWS // 2
BLOCK = 384
COLS = ((0, 512), (512, 512), (1024, 384))
f32, bf16 = jnp.float32, jnp.bfloat16
NT = (((1,), (1,)), ((), ()))


def dot(a, b):
    return jnp.dot(a, b, preferred_element_type=f32)


def dot_nt(a, b):
    return lax.dot_general(a, b, NT, preferred_element_type=f32)


def split(x):
    hi = x.astype(bf16)
    return hi, (x - hi.astype(f32)).astype(bf16)


def eliminate(grams, y_ref):
    row = lax.broadcasted_iota(jnp.int32, (R, 2 * R), 0)
    lane = lax.broadcasted_iota(jnp.int32, (R, 2 * R), 1)
    eye = jnp.where(lane == row + 64, 1.0, 0.0)
    unit = jnp.where(lane == row, 1.0, 0.0)
    for m in range(8):
        if m < MATS:
            gram = grams[m // 2]
            gram = pltpu.roll(gram, 64, axis=1) if m % 2 else gram
        else:
            gram = unit
        y_ref[pl.ds(m, R, stride=8), :] = jnp.where(lane < 64, gram, eye)
    rows = [y_ref[8 * i : 8 * i + 8] for i in range(R)]

    def at(r, k):
        return jnp.broadcast_to(r[:, k : k + 1], (8, 128))

    for k in range(0, R, 4):
        r0, r1, r2, r3 = rows[k : k + 4]
        s00, s01, s02, s03 = (at(r0, k + i) for i in range(4))
        s11, s12, s13 = (at(r1, k + i) for i in range(1, 4))
        s22, s23, s33 = at(r2, k + 2), at(r2, k + 3), at(r3, k + 3)
        i0 = 1.0 / s00
        l10, l20, l30 = s01 * i0, s02 * i0, s03 * i0
        d1 = s11 - l10 * s01
        t12, t13 = s12 - l10 * s02, s13 - l10 * s03
        i1 = 1.0 / d1
        l21, l31 = t12 * i1, t13 * i1
        d2 = s22 - l20 * s02 - l21 * t12
        t23 = s23 - l20 * s03 - l21 * t13
        i2 = 1.0 / d2
        l32 = t23 * i2
        d3 = s33 - l30 * s03 - l31 * t13 - l32 * t23
        i3 = 1.0 / d3
        r1 = r1 - l10 * r0
        r2 = r2 - l20 * r0 - l21 * r1
        r3 = r3 - l30 * r0 - l31 * r1 - l32 * r2
        q0, q1, q2, q3 = r0 * i0, r1 * i1, r2 * i2, r3 * i3
        for i in range(k + 4, R):
            if i < k + 8:
                c0, c1, c2, c3 = (at(rows[i], k + j) for j in range(4))
                c1 = c1 - l10 * c0
                c2 = c2 - l20 * c0 - l21 * c1
                c3 = c3 - l30 * c0 - l31 * c1 - l32 * c2
            else:
                c0, c1, c2, c3 = at(r0, i), at(r1, i), at(r2, i), at(r3, i)
            rows[i] = rows[i] - (c0 * q0 + c1 * q1) - (c2 * q2 + c3 * q3)
        for i, (r, d) in enumerate(((r0, s00), (r1, d1), (r2, d2), (r3, d3))):
            y_ref[8 * (k + i) : 8 * (k + i) + 8] = r * (1.0 / jnp.sqrt(d))
        yield


def comm_kernel(
    g_hbm, e_hbm, q_hbm, g_sum, p_out, y_out, m_hbm,
    gbuf, ebuf, qbuf, mh, ml, qst, p_own, p_recv, p_chip, p_far, g_acc,
    core_recv, recv0, recv1, q_acc, x_acc, recv2, recv3, gram_own, gram_half, gram_recv, gram_out,
    load_sem, p_send, p_arrive, c_send, c_arrive, a_send, a_arrive, b_send, b_arrive,
    gram_send, gram_arrive, store_sem,
):
    dp, mp = lax.axis_index("dp"), lax.axis_index("mp")
    y_hi, core = lax.div(dp, 2), lax.rem(dp, 2)
    x = lax.rem(mp, 4)
    z = lax.rem(lax.div(mp, 4), 4)
    y = y_hi * 2 + lax.div(mp, 16)

    def device(xx, yy, zz, cc):
        return (lax.div(yy, 2) * 2 + cc, lax.rem(yy, 2) * 16 + zz * 4 + xx)

    def flip(v):
        return v + 1 - 2 * lax.rem(v, 2)

    def side0(v):
        hi = lax.div(v, 2)
        lo = lax.rem(v, 2)
        return hi + lo - 2 * hi * lo

    def side1(v):
        return lax.div(v, 2)

    def over(*links):
        xx, yy, zz = x, y, z
        for link in links:
            if link % 3 == 0:
                xx = flip(x) if link == 0 else 3 - x
            elif link % 3 == 1:
                yy = flip(y) if link == 1 else 3 - y
            else:
                zz = flip(z) if link == 2 else 3 - z
        return device(xx, yy, zz, core)

    near = tuple(over(link) for link in range(6))
    corner = tuple(over(link, (link + 1) % 6) for link in range(6))
    sides = (side0(x), side0(y), side0(z), side1(x), side1(y), side1(z))
    twin = device(x, y, z, 1 - core)
    far = device(x, lax.rem(y + 2, 4), z, core)

    loads = []
    for m in range(MATS):
        loads.append((
            pltpu.make_async_copy(q_hbm.at[m], qbuf.at[m], load_sem.at[m, 0]),
            pltpu.make_async_copy(g_hbm.at[0, m], gbuf.at[m], load_sem.at[m, 1]),
            pltpu.make_async_copy(e_hbm.at[0, m], ebuf.at[m], load_sem.at[m, 2]),
        ))
        for copy in loads[-1]:
            copy.start()

    barrier = pltpu.get_barrier_semaphore()
    everyone = near + corner + (twin, far)
    for other in everyone:
        pl.semaphore_signal(barrier, inc=1, device_id=other, device_id_type=MESH)

    def remote(src, dst, send, arrive, target):
        copy = pltpu.make_async_remote_copy(
            src_ref=src, dst_ref=dst, send_sem=send, recv_sem=arrive,
            device_id=target, device_id_type=MESH,
        )
        copy.start()
        return copy

    mine = pl.multiple_of(core * HALF, 8)
    theirs = pl.multiple_of((1 - core) * HALF, 8)
    stores = []
    qst[...] = jnp.zeros_like(qst)
    q_acc[...] = jnp.zeros_like(q_acc)

    def local_p(j):
        total = None
        for b in range(2):
            m = 2 * j + b
            for copy in loads[m]:
                copy.wait()

            def merge(i, _, m=m):
                rows = pl.ds(pl.multiple_of(i * 16, 16), 16)
                merged = gbuf[m, rows].astype(f32) + ebuf[m, rows]
                ebuf[m, rows] = merged
                hi, lo = split(merged)
                mh[m, rows] = hi
                ml[m, rows] = lo
                return 0

            lax.fori_loop(0, ROWS // 16, merge, 0)
            store = pltpu.make_async_copy(ebuf.at[m], m_hbm.at[m], store_sem.at[m])
            store.start()
            stores.append(store)
            hi, lo = split(qbuf[m])
            qst[b, 64 * b : 64 * b + 64] = hi
            qst[b, 128 + 64 * b : 192 + 64 * b] = lo
            wide = dot_nt(mh[m], qst[b])
            part = wide[:, :128] + wide[:, 128:] + dot_nt(ml[m], qst[b, :128])
            total = part if total is None else total + part
        p_own[j] = total

    def p_chain(j):
        copy = remote(p_own.at[j, pl.ds(theirs, HALF)], p_recv.at[j], p_send.at[0, j], p_arrive.at[0, j], twin)
        yield
        copy.wait()
        p_chip[j] = p_own[j, pl.ds(mine, HALF)] + p_recv[j]
        copy = remote(p_chip.at[j], p_far.at[j], p_send.at[1, j], p_arrive.at[1, j], far)
        yield
        copy.wait()
        p_out[j, pl.ds(mine, HALF)] = (p_chip[j] + p_far[j]) * 0.25
        part = p_out.at[j, pl.ds(mine, HALF)]
        copy = remote(part, part, p_send.at[2, j], p_arrive.at[2, j], twin)
        yield
        copy.wait()
        yield

    halves = {}

    def three(src, dst, send, arrive, link):
        targets = (near[(link + 1) % 6], near[link], corner[link])
        return [remote(src(f), dst.at[f], send.at[f], arrive.at[f], targets[f]) for f in range(3)]

    def gram_chain(j):
        halves[j] = hi, lo = split(p_out[j].T)
        square = dot_nt(hi, hi) + (dot_nt(hi, lo) + dot_nt(lo, hi))
        lane = lax.broadcasted_iota(jnp.int32, (R, 2 * R), 1)
        gram_own[j] = jnp.where(lane < 64, square[:64], square[64:])
        rows = pl.ds(pl.multiple_of(core * 32, 32), 32)
        gram_half[j, 0] = gram_own[j, rows]
        for s, link in enumerate((2, 5) if j % 2 == 0 else (5, 2)):
            copies = three(
                lambda f: gram_half.at[j, s], gram_recv.at[j, s], gram_send.at[j, s], gram_arrive.at[j, s], link,
            )
            yield
            for copy in copies:
                copy.wait()
            got = gram_recv.at[j, s]
            gram_half[j, s + 1] = (gram_half[j, s] + got[1]) + (got[0] + got[2])
        copy = remote(
            gram_half.at[j, 2], gram_recv.at[j, 2, 0], gram_send.at[j, 2, 0], gram_arrive.at[j, 2, 0], near[1],
        )
        yield
        copy.wait()
        gram_out[j, rows] = gram_half[j, 2] + gram_recv[j, 2, 0]
        part = gram_out.at[j, rows]
        copy = remote(part, part, gram_send.at[j, 2, 1], gram_arrive.at[j, 2, 1], twin)
        yield
        copy.wait()

    def local_g(m):
        j, b = divmod(m, 2)
        hi, lo = halves[j]
        top = hi[64 * b : 64 * b + 64]
        both = jnp.concatenate([top, lo[64 * b : 64 * b + 64]], axis=0)
        for start, size in COLS:
            cols = slice(start, start + size)
            wide = dot(both, mh[m, :, cols])
            g_acc[m, :, cols] = wide[:64] + wide[64:] + dot(top, ml[m, :, cols])

    def g_chain(m):
        link = [(m + s) % 6 for s in range(6)]
        keep = pl.multiple_of(core * 32, 32)
        give = pl.multiple_of((1 - core) * 32, 32)
        kept0 = pl.multiple_of(core * 32 + 16 * sides[link[0]], 16)
        gone0 = pl.multiple_of(core * 32 + 16 - 16 * sides[link[0]], 16)
        kept1 = pl.multiple_of(kept0 + 8 * sides[link[1]], 8)
        gone1 = pl.multiple_of(kept0 + 8 - 8 * sides[link[1]], 8)
        hi, lo = sides[link[2]], sides[link[3]]

        def block(h, l):
            return pl.ds(pl.multiple_of((2 * h + l) * BLOCK, 128), BLOCK)

        own = block(hi, lo)
        others = (block(hi, 1 - lo), block(1 - hi, lo), block(1 - hi, 1 - lo))

        def send(s, src, dst, i):
            return remote(src, dst, a_send.at[s, m], a_arrive.at[s, m], near[link[i]])

        def forward(i, row, size):
            part = g_sum.at[m, pl.ds(row, size), pl.ds(0, D)]
            return remote(part, part, c_send.at[i, m], c_arrive.at[i, m], twin)

        copy = remote(g_acc.at[m, pl.ds(give, 32)], core_recv.at[m], c_send.at[0, m], c_arrive.at[0, m], twin)
        yield
        copy.wait()
        g_acc[m, pl.ds(keep, 32)] += core_recv[m]
        copy = send(0, g_acc.at[m, pl.ds(gone0, 16)], recv0.at[m], 0)
        yield
        copy.wait()
        g_acc[m, pl.ds(kept0, 16)] += recv0[m]
        copy = send(1, g_acc.at[m, pl.ds(gone1, 8)], recv1.at[m], 1)
        yield
        copy.wait()
        q_acc[m, :, :D] = g_acc[m, pl.ds(kept1, 8)] + recv1[m]
        copies = three(lambda f: q_acc.at[m, :, others[f]], recv2.at[m], b_send.at[0, m], b_arrive.at[0, m], link[2])
        yield
        for copy in copies:
            copy.wait()
        x_acc[m] = (q_acc[m, :, own] + recv2[m, 1]) + (recv2[m, 0] + recv2[m, 2])
        copies = three(lambda f: x_acc.at[m], recv3.at[m], b_send.at[1, m], b_arrive.at[1, m], link[4])
        yield
        for copy in copies:
            copy.wait()
        g_sum[m, pl.ds(kept1, 8), own] = (x_acc[m] + recv3[m, 1]) + (recv3[m, 0] + recv3[m, 2])
        part = g_sum.at[m, pl.ds(kept1, 8), own]
        targets = (near[link[3]], near[link[2]], corner[link[2]])
        copies = [remote(part, part, b_send.at[2, m, f], b_arrive.at[2, m, f], targets[f]) for f in range(3)]
        yield
        for copy in copies:
            copy.wait()
        part = g_sum.at[m, pl.ds(kept1, 8), pl.ds(0, D)]
        copy = send(2, part, part, 1)
        passed = [forward(1, kept1, 8)]
        yield
        copy.wait()
        part = g_sum.at[m, pl.ds(kept0, 16), pl.ds(0, D)]
        copy = send(3, part, part, 0)
        passed.append(forward(2, gone1, 8))
        yield
        copy.wait()
        passed.append(forward(3, gone0, 16))
        yield
        for copy in passed:
            copy.wait()

    pc = [p_chain(j) for j in range(3)]
    gc = [gram_chain(j) for j in range(3)]
    ac = [g_chain(m) for m in range(MATS)]
    factor = None

    def behind():
        nonlocal factor
        if factor is None:
            if all([next(chain, 1) for chain in gc]):
                factor = eliminate([gram_out[j] for j in range(3)], y_out)
        if factor is not None:
            next(factor, None)

    local_p(0)
    pl.semaphore_wait(barrier, len(everyone))
    next(pc[0])
    local_p(1)
    next(pc[1])
    next(pc[0])
    local_p(2)
    next(pc[2])
    next(pc[1])
    next(pc[0])
    next(pc[2])
    next(pc[0])
    next(gc[0])
    local_g(0)
    next(ac[0])
    next(pc[1])
    local_g(1)
    next(ac[1])
    next(pc[2])
    next(pc[1])
    next(gc[1])
    next(gc[0])
    local_g(2)
    next(ac[2])
    next(ac[0])
    local_g(3)
    next(ac[3])
    next(ac[1])
    next(pc[2])
    next(gc[2])
    next(gc[1])
    next(gc[0])
    local_g(4)
    next(ac[4])
    next(ac[2])
    local_g(5)
    next(ac[5])
    next(ac[3])
    next(gc[2])
    next(gc[1])
    next(gc[0])
    next(ac[4])
    next(ac[5])
    for s in range(8):
        for m in range(MATS):
            next(ac[m], None)
            if factor is not None or m in (2, 5):
                behind()
    for _ in factor:
        pass
    for store in stores:
        store.wait()


def finish_kernel(
    g_sum, p_ref, y_ref, m_hbm, err_hbm, q_out, mbuf, new_q, wst, load_sem, store_sem, q_sem,
):
    loads = [pltpu.make_async_copy(m_hbm.at[m], mbuf.at[m], load_sem.at[m]) for m in range(MATS)]
    for copy in loads:
        copy.start()
    lane = lax.broadcasted_iota(jnp.int32, (R, 2 * R), 1)
    wide_lane = lax.broadcasted_iota(jnp.int32, (ROWS, 2 * R), 1)
    stores = []
    for m in range(MATS):
        b = m % 2
        side = jnp.where(lane >= 64, y_ref[pl.ds(m, R, stride=8), :], 0.0)
        other = pltpu.roll(side, 64, axis=1)
        inverse = side if b else other
        bh, bl = split(jnp.concatenate([inverse, inverse], axis=0))
        ph, pl_ = split(p_ref[m // 2])
        ortho = dot_nt(ph, bh) + (dot_nt(ph, bl) + dot_nt(pl_, bh))
        oh, ol = split(ortho)
        lhs = jnp.concatenate([jnp.where(wide_lane < 64, oh, ol), oh[:, :64]], axis=1)
        lh, ll = split(side + other)
        lhs_q = jnp.concatenate([jnp.where(lane < 64, lh, ll), lh[:, :64]], axis=1)
        gh, gl = split(g_sum[m, :, :D] * 0.25)
        wst[0, 0:64] = gh
        wst[0, 64:128] = gh
        wst[0, 128:192] = gl
        fresh = dot(lhs_q, wst[0])
        new_q[m] = fresh
        store = pltpu.make_async_copy(new_q.at[m], q_out.at[m], q_sem.at[m])
        store.start()
        stores.append(store)
        nh, nl = split(fresh)
        wst[1, 0:64] = nh
        wst[1, 64:128] = nh
        wst[1, 128:192] = nl
        loads[m].wait()
        for start, size in COLS:
            cols = slice(start, start + size)
            mbuf[m, :, cols] = mbuf[m, :, cols] - dot(lhs, wst[1, :, cols])
        store = pltpu.make_async_copy(mbuf.at[m], err_hbm.at[0, m], store_sem.at[m])
        store.start()
        stores.append(store)
    for store in stores:
        store.wait()


def body(gradients, errors, previous_q):
    vmem, hbm = pl.BlockSpec(memory_space=pltpu.VMEM), pl.BlockSpec(memory_space=pl.ANY)
    far_hbm = pl.BlockSpec(memory_space=pltpu.HBM)
    sem = pltpu.SemaphoreType.DMA
    g_sum, p_mat, y_mat, merged = pl.pallas_call(
        comm_kernel,
        out_shape=(
            jax.ShapeDtypeStruct((MATS, R, 4 * BLOCK), f32),
            jax.ShapeDtypeStruct((MATS // 2, ROWS, 2 * R), f32),
            jax.ShapeDtypeStruct((8 * R, 2 * R), f32),
            jax.ShapeDtypeStruct((MATS, ROWS, D), f32),
        ),
        in_specs=[far_hbm, far_hbm, far_hbm],
        out_specs=(vmem, vmem, vmem, hbm),
        scratch_shapes=[
            pltpu.VMEM((MATS, ROWS, D), bf16),
            pltpu.VMEM((MATS, ROWS, D), f32),
            pltpu.VMEM((MATS, R, D), f32),
            pltpu.VMEM((MATS, ROWS, D), bf16),
            pltpu.VMEM((MATS, ROWS, D), bf16),
            pltpu.VMEM((2, 256, D), bf16),
            pltpu.VMEM((MATS // 2, ROWS, 128), f32),
            pltpu.VMEM((MATS // 2, HALF, 128), f32),
            pltpu.VMEM((MATS // 2, HALF, 128), f32),
            pltpu.VMEM((MATS // 2, HALF, 128), f32),
            pltpu.VMEM((MATS, R, D), f32),
            pltpu.VMEM((MATS, 32, D), f32),
            pltpu.VMEM((MATS, 16, D), f32),
            pltpu.VMEM((MATS, 8, D), f32),
            pltpu.VMEM((MATS, 8, 4 * BLOCK), f32),
            pltpu.VMEM((MATS, 8, BLOCK), f32),
            pltpu.VMEM((MATS, 3, 8, BLOCK), f32),
            pltpu.VMEM((MATS, 3, 8, BLOCK), f32),
            pltpu.VMEM((MATS // 2, R, 2 * R), f32),
            pltpu.VMEM((MATS // 2, 3, R // 2, 2 * R), f32),
            pltpu.VMEM((MATS // 2, 3, 3, R // 2, 2 * R), f32),
            pltpu.VMEM((MATS // 2, R, 2 * R), f32),
            sem((MATS, 3)),
            sem((3, 3)),
            sem((3, 3)),
            sem((4, MATS)),
            sem((4, MATS)),
            sem((4, MATS)),
            sem((4, MATS)),
            sem((3, MATS, 3)),
            sem((3, MATS, 3)),
            sem((3, 3, 3)),
            sem((3, 3, 3)),
            sem((MATS,)),
        ],
        compiler_params=pltpu.CompilerParams(
            collective_id=0, has_side_effects=True, vmem_limit_bytes=40 * 2**20
        ),
        name="compress_and_sum",
    )(*[pltpu.with_memory_space_constraint(v, pltpu.HBM) for v in (gradients, errors, previous_q)])
    return pl.pallas_call(
        finish_kernel,
        out_shape=(
            jax.ShapeDtypeStruct((1, MATS, ROWS, D), f32),
            jax.ShapeDtypeStruct((MATS, R, D), f32),
        ),
        in_specs=[vmem, vmem, vmem, hbm],
        out_specs=(far_hbm, far_hbm),
        scratch_shapes=[
            pltpu.VMEM((MATS, ROWS, D), f32),
            pltpu.VMEM((MATS, R, D), f32),
            pltpu.VMEM((2, ROWS, D), bf16),
            sem((MATS,)),
            sem((MATS,)),
            sem((MATS,)),
        ],
        compiler_params=pltpu.CompilerParams(vmem_limit_bytes=24 * 2**20),
        name="new_q_and_errors",
    )(g_sum, p_mat, y_mat, merged)


def solution(mesh):
    in_specs = (P("dp", None, "mp", None), P("dp", None, "mp", None), P())
    out_specs = (P("dp", None, "mp", None), P())
    return jax.shard_map(body, mesh=mesh, in_specs=in_specs, out_specs=out_specs, check_vma=False)
```

time: 663 us -> 64 us (0.10)
  waiting for transfers between devices: 491 us -> 0 us
  other arithmetic: 84.2 us -> 0 us
  matrix products: 63.4 us -> 0 us
  Pallas kernels: 0 us -> 63.3 us
  between operations: 14.2 us -> 0.64 us
  local copies, waits for them, and re-layouts: 8.24 us -> 0 us
    psum x3 -> x0, waiting for transfers between devices: 491 us -> none  [the longest x1 275 us: body(): gram_mat = lax.psum(jnp.dot(p_mat.T, p_mat, precision=exact_mode), 'mp')]
    another operation x31 -> x0, other arithmetic: 78.3 us -> none  [the longest x18 42.3 us: body(): factor = jnp.linalg.cholesky(gram_mat)]
    pallas_call x0 -> x2, Pallas kernels: none -> 63.3 us  [the longest x1 58.5 us: body(): pl.pallas_call(comm_kernel, out_shape=(jax.ShapeDtypeStruct((MATS, R, 4 *...]
    dot_general x24 -> x0, matrix products: 57.7 us -> none  [the longest x6 19.6 us: body(): lax.dot_general(merged, previous_q[which], (((1,), (1,)), ((), ())), prec...]
  transfers between devices with their start and end apart: 3 -> 0, of which waited for: 3 -> 0; matrix products, arithmetic and copies ran while one was open for 0% -> 0% of each run, Pallas kernels for 0% -> 0%
where the time goes in v1:
time: 64 us; the launch traced here: 63.9 us
  Pallas kernels  63.3 us (99%)
  between operations  0.64 us (1%)
    pallas_call x1, Pallas kernels, body(): pl.pallas_call(comm_kernel, out_shape=(jax.ShapeDtypeStruct((MATS, R, 4 *...  58.5 us
    pallas_call x1, Pallas kernels, body(): pl.pallas_call(finish_kernel, out_shape=(jax.ShapeDtypeStruct((1, MATS, R...  4.77 us

profile of v1, /device:TPU:1, one launch (start us, length us, event | category | flops | bytes accessed | tf_op | source)
XLA Modules:
  0.0 63.9 jit_solution(6115865174168508138)
XLA Ops:
  0.6 58.5 %compress_and_sum.1 = (f32[6,64,1536]{2,1,0:T(8,128)S(1)}, f32[3,192,128]{2,1,0:T(8,128)S(1)}, f32[512,128]{1,0:T(8,128)S(1)}, f32[6,192,1408]{2,1,0:T(8,128)S(1)}) custom-call(bf16[1,6,192,1408]{3,2,1,0:T(8,128)(2,1)} %g_hbm.1, f32[1,6,192,1408]{3,2,1,0:T(8,128)} %e_hbm.1, f32[6,64,1408]{2,1,0:T(8,128)} %q_hbm.1), custom_call_target="tpu_custom_call" | custom-call | tf_op jit(solution)/shard_map/compress_and_sum/pallas_call | solution.py:425
  59.2 4.8 %new_q_and_errors.1 = (f32[1,6,192,1408]{3,2,1,0:T(8,128)}, f32[6,64,1408]{2,1,0:T(8,128)}) custom-call(f32[6,64,1536]{2,1,0:T(8,128)S(1)} %get-tuple-element.6.g_sum, f32[3,192,128]{2,1,0:T(8,128)S(1)} %get-tuple-element.7.p_ref, f32[512,128]{1,0:T(8,128)S(1)} %get-tuple-element.8.y_ref, f32[6,192,1408]{2,1,0:T(8,128)S(1)} %get-tuple-element.9.m_hbm), custom_call_target="tpu_custom_call" | custom-call | tf_op jit(solution)/shard_map/new_q_and_errors/pallas_call | solution.py:476

commit v2 on v1

--- a/solution.py
+++ b/solution.py
@@ -125,16 +125,22 @@
     twin = device(x, y, z, 1 - core)
     far = device(x, lax.rem(y + 2, 4), z, core)
 
-    loads = []
-    for m in range(MATS):
-        loads.append((
+    def loads(m):
+        return (
             pltpu.make_async_copy(q_hbm.at[m], qbuf.at[m], load_sem.at[m, 0]),
             pltpu.make_async_copy(g_hbm.at[0, m], gbuf.at[m], load_sem.at[m, 1]),
             pltpu.make_async_copy(e_hbm.at[0, m], ebuf.at[m], load_sem.at[m, 2]),
-        ))
-        for copy in loads[-1]:
+        )
+
+    def store(m):
+        return pltpu.make_async_copy(ebuf.at[m], m_hbm.at[m], store_sem.at[m])
+
+    def begin(m, _):
+        for copy in loads(m):
             copy.start()
-
+        return 0
+
+    lax.fori_loop(0, MATS, begin, 0)
     barrier = pltpu.get_barrier_semaphore()
     everyone = near + corner + (twin, far)
     for other in everyone:
@@ -150,52 +156,76 @@
 
     mine = pl.multiple_of(core * HALF, 8)
     theirs = pl.multiple_of((1 - core) * HALF, 8)
-    stores = []
+    p_own[...] = jnp.zeros_like(p_own)
     qst[...] = jnp.zeros_like(qst)
     q_acc[...] = jnp.zeros_like(q_acc)
 
-    def local_p(j):
-        total = None
-        for b in range(2):
-            m = 2 * j + b
-            for copy in loads[m]:
-                copy.wait()
-
-            def merge(i, _, m=m):
-                rows = pl.ds(pl.multiple_of(i * 16, 16), 16)
-                merged = gbuf[m, rows].astype(f32) + ebuf[m, rows]
-                ebuf[m, rows] = merged
-                hi, lo = split(merged)
-                mh[m, rows] = hi
-                ml[m, rows] = lo
-                return 0
-
-            lax.fori_loop(0, ROWS // 16, merge, 0)
-            store = pltpu.make_async_copy(ebuf.at[m], m_hbm.at[m], store_sem.at[m])
-            store.start()
-            stores.append(store)
-            hi, lo = split(qbuf[m])
-            qst[b, 64 * b : 64 * b + 64] = hi
-            qst[b, 128 + 64 * b : 192 + 64 * b] = lo
-            wide = dot_nt(mh[m], qst[b])
-            part = wide[:, :128] + wide[:, 128:] + dot_nt(ml[m], qst[b, :128])
-            total = part if total is None else total + part
-        p_own[j] = total
-
-    def p_chain(j):
-        copy = remote(p_own.at[j, pl.ds(theirs, HALF)], p_recv.at[j], p_send.at[0, j], p_arrive.at[0, j], twin)
-        yield
-        copy.wait()
-        p_chip[j] = p_own[j, pl.ds(mine, HALF)] + p_recv[j]
-        copy = remote(p_chip.at[j], p_far.at[j], p_send.at[1, j], p_arrive.at[1, j], far)
-        yield
-        copy.wait()
-        p_out[j, pl.ds(mine, HALF)] = (p_chip[j] + p_far[j]) * 0.25
-        part = p_out.at[j, pl.ds(mine, HALF)]
-        copy = remote(part, part, p_send.at[2, j], p_arrive.at[2, j], twin)
-        yield
-        copy.wait()
-        yield
+    def local_p(m):
+        b = lax.rem(m, 2)
+        for copy in loads(m):
+            copy.wait()
+
+        def merge(i, _):
+            rows = pl.ds(pl.multiple_of(i * 32, 32), 32)
+            merged = gbuf[m, rows].astype(f32) + ebuf[m, rows]
+            ebuf[m, rows] = merged
+            hi, lo = split(merged)
+            mh[m, rows] = hi
+            ml[m, rows] = lo
+            return 0
+
+        lax.fori_loop(0, ROWS // 32, merge, 0)
+        store(m).start()
+        hi, lo = split(qbuf[m])
+        at = pl.multiple_of(64 * b, 64)
+        qst[b, pl.ds(at, 64)] = hi
+        qst[b, pl.ds(at + 128, 64)] = lo
+        wide = dot_nt(mh[m], qst[b])
+        p_own[lax.div(m, 2)] += wide[:, :128] + wide[:, 128:] + dot_nt(ml[m], qst[b, :128])
+
+    def p_copy(s, j):
+        if s == 0:
+            src, dst, target = p_own.at[j, pl.ds(theirs, HALF)], p_recv.at[j], twin
+        elif s == 1:
+            src, dst, target = p_chip.at[j], p_far.at[j], far
+        else:
+            src = dst = p_out.at[j, pl.ds(mine, HALF)]
+            target = twin
+        return pltpu.make_async_remote_copy(
+            src_ref=src, dst_ref=dst, send_sem=p_send.at[s, j], recv_sem=p_arrive.at[s, j],
+            device_id=target, device_id_type=MESH,
+        )
+
+    def p_step(s, j):
+        if s > 0:
+            p_copy(s - 1, j).wait()
+        if s == 1:
+            p_chip[j] = p_own[j, pl.ds(mine, HALF)] + p_recv[j]
+        if s == 2:
+            p_out[j, pl.ds(mine, HALF)] = (p_chip[j] + p_far[j]) * 0.25
+        if s < 3:
+            p_copy(s, j).start()
+
+    def p_loop(m, _):
+        local_p(m)
+
+        @pl.when(m == 1)
+        def _():
+            pl.semaphore_wait(barrier, len(everyone))
+            p_step(0, 0)
+
+        @pl.when(m == 3)
+        def _():
+            p_step(0, 1)
+            p_step(1, 0)
+
+        @pl.when(m == 5)
+        def _():
+            p_step(0, 2)
+            p_step(1, 1)
+            p_step(2, 0)
+
+        return 0
 
     halves = {}
 
@@ -306,7 +336,6 @@
         for copy in passed:
             copy.wait()
 
-    pc = [p_chain(j) for j in range(3)]
     gc = [gram_chain(j) for j in range(3)]
     ac = [g_chain(m) for m in range(MATS)]
     factor = None
@@ -319,26 +348,17 @@
         if factor is not None:
             next(factor, None)
 
-    local_p(0)
-    pl.semaphore_wait(barrier, len(everyone))
-    next(pc[0])
-    local_p(1)
-    next(pc[1])
-    next(pc[0])
-    local_p(2)
-    next(pc[2])
-    next(pc[1])
-    next(pc[0])
-    next(pc[2])
-    next(pc[0])
+    lax.fori_loop(0, MATS, p_loop, 0)
+    p_step(1, 2)
+    p_step(3, 0)
     next(gc[0])
     local_g(0)
     next(ac[0])
-    next(pc[1])
+    p_step(2, 1)
     local_g(1)
     next(ac[1])
-    next(pc[2])
-    next(pc[1])
+    p_step(2, 2)
+    p_step(3, 1)
     next(gc[1])
     next(gc[0])
     local_g(2)
@@ -347,7 +367,7 @@
     local_g(3)
     next(ac[3])
     next(ac[1])
-    next(pc[2])
+    p_step(3, 2)
     next(gc[2])
     next(gc[1])
     next(gc[0])
@@ -369,30 +389,45 @@
                 behind()
     for _ in factor:
         pass
-    for store in stores:
-        store.wait()
+    for m in range(MATS):
+        store(m).wait()
 
 
 def finish_kernel(
     g_sum, p_ref, y_ref, m_hbm, err_hbm, q_out, mbuf, new_q, wst, load_sem, store_sem, q_sem,
 ):
-    loads = [pltpu.make_async_copy(m_hbm.at[m], mbuf.at[m], load_sem.at[m]) for m in range(MATS)]
-    for copy in loads:
-        copy.start()
+    def load(m):
+        return pltpu.make_async_copy(m_hbm.at[m], mbuf.at[m], load_sem.at[m])
+
+    def store_q(m):
+        return pltpu.make_async_copy(new_q.at[m], q_out.at[m], q_sem.at[m])
+
+    def store_err(m):
+        return pltpu.make_async_copy(mbuf.at[m], err_hbm.at[0, m], store_sem.at[m])
+
+    def begin(m, _):
+        load(m).start()
+        return 0
+
+    def end(m, _):
+        store_q(m).wait()
+        store_err(m).wait()
+        return 0
+
     lane = lax.broadcasted_iota(jnp.int32, (R, 2 * R), 1)
     wide_lane = lax.broadcasted_iota(jnp.int32, (ROWS, 2 * R), 1)
-    stores = []
-    for m in range(MATS):
-        b = m % 2
+
+    def step(m, _):
+        b = lax.rem(m, 2)
         side = jnp.where(lane >= 64, y_ref[pl.ds(m, R, stride=8), :], 0.0)
-        other = pltpu.roll(side, 64, axis=1)
-        inverse = side if b else other
+        both = side + pltpu.roll(side, 64, axis=1)
+        inverse = jnp.where((lane >= 64) == (b == 1), both, 0.0)
         bh, bl = split(jnp.concatenate([inverse, inverse], axis=0))
-        ph, pl_ = split(p_ref[m // 2])
+        ph, pl_ = split(p_ref[lax.div(m, 2)])
         ortho = dot_nt(ph, bh) + (dot_nt(ph, bl) + dot_nt(pl_, bh))
         oh, ol = split(ortho)
         lhs = jnp.concatenate([jnp.where(wide_lane < 64, oh, ol), oh[:, :64]], axis=1)
-        lh, ll = split(side + other)
+        lh, ll = split(both)
         lhs_q = jnp.concatenate([jnp.where(lane < 64, lh, ll), lh[:, :64]], axis=1)
         gh, gl = split(g_sum[m, :, :D] * 0.25)
         wst[0, 0:64] = gh
@@ -400,22 +435,21 @@
         wst[0, 128:192] = gl
         fresh = dot(lhs_q, wst[0])
         new_q[m] = fresh
-        store = pltpu.make_async_copy(new_q.at[m], q_out.at[m], q_sem.at[m])
-        store.start()
-        stores.append(store)
+        store_q(m).start()
         nh, nl = split(fresh)
         wst[1, 0:64] = nh
         wst[1, 64:128] = nh
         wst[1, 128:192] = nl
-        loads[m].wait()
+        load(m).wait()
         for start, size in COLS:
             cols = slice(start, start + size)
             mbuf[m, :, cols] = mbuf[m, :, cols] - dot(lhs, wst[1, :, cols])
-        store = pltpu.make_async_copy(mbuf.at[m], err_hbm.at[0, m], store_sem.at[m])
-        store.start()
-        stores.append(store)
-    for store in stores:
-        store.wait()
+        store_err(m).start()
+        return 0
+
+    lax.fori_loop(0, MATS, begin, 0)
+    lax.fori_loop(0, MATS, step, 0)
+    lax.fori_loop(0, MATS, end, 0)
 
 
 def body(gradients, errors, previous_q):

time: 64 us -> 65.3 us (1.020)
  Pallas kernels: 63.3 us -> 64.6 us
    pallas_call x1, Pallas kernels: 4.77 us -> 5.86 us  [body(): pl.pallas_call(finish_kernel, out_shape=(jax.ShapeDtypeStruct((1, MATS, R...]
where the time goes in v2:
time: 65.3 us; the launch traced here: 65.2 us
  Pallas kernels  64.6 us (99%)
    pallas_call x1, Pallas kernels, body(): pl.pallas_call(comm_kernel, out_shape=(jax.ShapeDtypeStruct((MATS, R, 4 *...  58.7 us
    pallas_call x1, Pallas kernels, body(): pl.pallas_call(finish_kernel, out_shape=(jax.ShapeDtypeStruct((1, MATS, R...  5.86 us

profile of v2, /device:TPU:1, one launch (start us, length us, event | category | flops | bytes accessed | tf_op | source)
XLA Modules:
  0.0 65.2 jit_solution(5409222506999008145)
XLA Ops:
  0.6 58.7 %compress_and_sum.1 = (f32[6,64,1536]{2,1,0:T(8,128)S(1)}, f32[3,192,128]{2,1,0:T(8,128)S(1)}, f32[512,128]{1,0:T(8,128)S(1)}, f32[6,192,1408]{2,1,0:T(8,128)S(1)}) custom-call(bf16[1,6,192,1408]{3,2,1,0:T(8,128)(2,1)} %g_hbm.1, f32[1,6,192,1408]{3,2,1,0:T(8,128)} %e_hbm.1, f32[6,64,1408]{2,1,0:T(8,128)} %q_hbm.1), custom_call_target="tpu_custom_call" | custom-call | tf_op jit(solution)/shard_map/compress_and_sum/pallas_call | solution.py:459
  59.3 5.9 %new_q_and_errors.1 = (f32[1,6,192,1408]{3,2,1,0:T(8,128)}, f32[6,64,1408]{2,1,0:T(8,128)}) custom-call(f32[6,64,1536]{2,1,0:T(8,128)S(1)} %get-tuple-element.6.g_sum, f32[3,192,128]{2,1,0:T(8,128)S(1)} %get-tuple-element.7.p_ref, f32[512,128]{1,0:T(8,128)S(1)} %get-tuple-element.8.y_ref, f32[6,192,1408]{2,1,0:T(8,128)S(1)} %get-tuple-element.9.m_hbm), custom_call_target="tpu_custom_call" | custom-call | tf_op jit(solution)/shard_map/new_q_and_errors/pallas_call | solution.py:510

commit v3 on v2

--- a/solution.py
+++ b/solution.py
@@ -82,11 +82,11 @@
 
 
 def comm_kernel(
-    g_hbm, e_hbm, q_hbm, g_sum, p_out, y_out, m_hbm,
-    gbuf, ebuf, qbuf, mh, ml, qst, p_own, p_recv, p_chip, p_far, g_acc,
+    g_hbm, e_hbm, q_hbm, g_sum, p_out, y_out, ebuf,
+    gbuf, qbuf, mh, ml, qst, p_own, p_recv, p_chip, p_far, g_acc,
     core_recv, recv0, recv1, q_acc, x_acc, recv2, recv3, gram_own, gram_half, gram_recv, gram_out,
     load_sem, p_send, p_arrive, c_send, c_arrive, a_send, a_arrive, b_send, b_arrive,
-    gram_send, gram_arrive, store_sem,
+    gram_send, gram_arrive,
 ):
     dp, mp = lax.axis_index("dp"), lax.axis_index("mp")
     y_hi, core = lax.div(dp, 2), lax.rem(dp, 2)
@@ -132,9 +132,6 @@
             pltpu.make_async_copy(e_hbm.at[0, m], ebuf.at[m], load_sem.at[m, 2]),
         )
 
-    def store(m):
-        return pltpu.make_async_copy(ebuf.at[m], m_hbm.at[m], store_sem.at[m])
-
     def begin(m, _):
         for copy in loads(m):
             copy.start()
@@ -175,7 +172,6 @@
             return 0
 
         lax.fori_loop(0, ROWS // 32, merge, 0)
-        store(m).start()
         hi, lo = split(qbuf[m])
         at = pl.multiple_of(64 * b, 64)
         qst[b, pl.ds(at, 64)] = hi
@@ -389,45 +385,25 @@
                 behind()
     for _ in factor:
         pass
-    for m in range(MATS):
-        store(m).wait()
 
 
 def finish_kernel(
-    g_sum, p_ref, y_ref, m_hbm, err_hbm, q_out, mbuf, new_q, wst, load_sem, store_sem, q_sem,
+    g_sum, p_ref, y_ref, m_ref, err_hbm, q_out, mbuf, new_q, wst, store_sem, q_sem,
 ):
-    def load(m):
-        return pltpu.make_async_copy(m_hbm.at[m], mbuf.at[m], load_sem.at[m])
-
-    def store_q(m):
-        return pltpu.make_async_copy(new_q.at[m], q_out.at[m], q_sem.at[m])
-
-    def store_err(m):
-        return pltpu.make_async_copy(mbuf.at[m], err_hbm.at[0, m], store_sem.at[m])
-
-    def begin(m, _):
-        load(m).start()
-        return 0
-
-    def end(m, _):
-        store_q(m).wait()
-        store_err(m).wait()
-        return 0
-
     lane = lax.broadcasted_iota(jnp.int32, (R, 2 * R), 1)
     wide_lane = lax.broadcasted_iota(jnp.int32, (ROWS, 2 * R), 1)
-
-    def step(m, _):
-        b = lax.rem(m, 2)
+    stores = []
+    for m in range(MATS):
+        b = m % 2
         side = jnp.where(lane >= 64, y_ref[pl.ds(m, R, stride=8), :], 0.0)
-        both = side + pltpu.roll(side, 64, axis=1)
-        inverse = jnp.where((lane >= 64) == (b == 1), both, 0.0)
+        other = pltpu.roll(side, 64, axis=1)
+        inverse = side if b else other
         bh, bl = split(jnp.concatenate([inverse, inverse], axis=0))
-        ph, pl_ = split(p_ref[lax.div(m, 2)])
+        ph, pl_ = split(p_ref[m // 2])
         ortho = dot_nt(ph, bh) + (dot_nt(ph, bl) + dot_nt(pl_, bh))
         oh, ol = split(ortho)
         lhs = jnp.concatenate([jnp.where(wide_lane < 64, oh, ol), oh[:, :64]], axis=1)
-        lh, ll = split(both)
+        lh, ll = split(side + other)
         lhs_q = jnp.concatenate([jnp.where(lane < 64, lh, ll), lh[:, :64]], axis=1)
         gh, gl = split(g_sum[m, :, :D] * 0.25)
         wst[0, 0:64] = gh
@@ -435,25 +411,25 @@
         wst[0, 128:192] = gl
         fresh = dot(lhs_q, wst[0])
         new_q[m] = fresh
-        store_q(m).start()
+        store = pltpu.make_async_copy(new_q.at[m], q_out.at[m], q_sem.at[m])
+        store.start()
+        stores.append(store)
         nh, nl = split(fresh)
         wst[1, 0:64] = nh
         wst[1, 64:128] = nh
         wst[1, 128:192] = nl
-        load(m).wait()
         for start, size in COLS:
             cols = slice(start, start + size)
-            mbuf[m, :, cols] = mbuf[m, :, cols] - dot(lhs, wst[1, :, cols])
-        store_err(m).start()
-        return 0
-
-    lax.fori_loop(0, MATS, begin, 0)
-    lax.fori_loop(0, MATS, step, 0)
-    lax.fori_loop(0, MATS, end, 0)
+            mbuf[m, :, cols] = m_ref[m, :, cols] - dot(lhs, wst[1, :, cols])
+        store = pltpu.make_async_copy(mbuf.at[m], err_hbm.at[0, m], store_sem.at[m])
+        store.start()
+        stores.append(store)
+    for store in stores:
+        store.wait()
 
 
 def body(gradients, errors, previous_q):
-    vmem, hbm = pl.BlockSpec(memory_space=pltpu.VMEM), pl.BlockSpec(memory_space=pl.ANY)
+    vmem = pl.BlockSpec(memory_space=pltpu.VMEM)
     far_hbm = pl.BlockSpec(memory_space=pltpu.HBM)
     sem = pltpu.SemaphoreType.DMA
     g_sum, p_mat, y_mat, merged = pl.pallas_call(
@@ -465,10 +441,9 @@
             jax.ShapeDtypeStruct((MATS, ROWS, D), f32),
         ),
         in_specs=[far_hbm, far_hbm, far_hbm],
-        out_specs=(vmem, vmem, vmem, hbm),
+        out_specs=(vmem, vmem, vmem, vmem),
         scratch_shapes=[
             pltpu.VMEM((MATS, ROWS, D), bf16),
-            pltpu.VMEM((MATS, ROWS, D), f32),
             pltpu.VMEM((MATS, R, D), f32),
             pltpu.VMEM((MATS, ROWS, D), bf16),
             pltpu.VMEM((MATS, ROWS, D), bf16),
@@ -500,7 +475,6 @@
             sem((3, MATS, 3)),
             sem((3, 3, 3)),
             sem((3, 3, 3)),
-            sem((MATS,)),
         ],
         compiler_params=pltpu.CompilerParams(
             collective_id=0, has_side_effects=True, vmem_limit_bytes=40 * 2**20
@@ -513,7 +487,7 @@
             jax.ShapeDtypeStruct((1, MATS, ROWS, D), f32),
             jax.ShapeDtypeStruct((MATS, R, D), f32),
         ),
-        in_specs=[vmem, vmem, vmem, hbm],
+        in_specs=[vmem, vmem, vmem, vmem],
         out_specs=(far_hbm, far_hbm),
         scratch_shapes=[
             pltpu.VMEM((MATS, ROWS, D), f32),
@@ -521,7 +495,6 @@
             pltpu.VMEM((2, ROWS, D), bf16),
             sem((MATS,)),
             sem((MATS,)),
-            sem((MATS,)),
         ],
         compiler_params=pltpu.CompilerParams(vmem_limit_bytes=24 * 2**20),
         name="new_q_and_errors",

time: 65.3 us -> 62.8 us (0.962)
  Pallas kernels: 64.6 us -> 62.1 us
    pallas_call x1, Pallas kernels: 5.86 us -> 4.05 us  [body(): pl.pallas_call(finish_kernel, out_shape=(jax.ShapeDtypeStruct((1, MATS, R...]
    pallas_call x1, Pallas kernels: 58.7 us -> 58 us  [body(): pl.pallas_call(comm_kernel, out_shape=(jax.ShapeDtypeStruct((MATS, R, 4 *...]
where the time goes in v3:
time: 62.8 us; the launch traced here: 62.7 us
  Pallas kernels  62.1 us (99%)
  between operations  0.64 us (1%)
    pallas_call x1, Pallas kernels, body(): pl.pallas_call(comm_kernel, out_shape=(jax.ShapeDtypeStruct((MATS, R, 4 *...  58 us
    pallas_call x1, Pallas kernels, body(): pl.pallas_call(finish_kernel, out_shape=(jax.ShapeDtypeStruct((1, MATS, R...  4.05 us

profile of v3, /device:TPU:1, one launch (start us, length us, event | category | flops | bytes accessed | tf_op | source)
XLA Modules:
  0.0 62.7 jit_solution(6632347032337908648)
XLA Ops:
  0.6 58.0 %compress_and_sum.1 = (f32[6,64,1536]{2,1,0:T(8,128)S(1)}, f32[3,192,128]{2,1,0:T(8,128)S(1)}, f32[512,128]{1,0:T(8,128)S(1)}, f32[6,192,1408]{2,1,0:T(8,128)S(1)}) custom-call(bf16[1,6,192,1408]{3,2,1,0:T(8,128)(2,1)} %g_hbm.1, f32[1,6,192,1408]{3,2,1,0:T(8,128)} %e_hbm.1, f32[6,64,1408]{2,1,0:T(8,128)} %q_hbm.1), custom_call_target="tpu_custom_call" | custom-call | tf_op jit(solution)/shard_map/compress_and_sum/pallas_call | solution.py:435
  58.6 4.1 %new_q_and_errors.1 = (f32[1,6,192,1408]{3,2,1,0:T(8,128)}, f32[6,64,1408]{2,1,0:T(8,128)}) custom-call(f32[6,64,1536]{2,1,0:T(8,128)S(1)} %get-tuple-element.6.g_sum, f32[3,192,128]{2,1,0:T(8,128)S(1)} %get-tuple-element.7.p_ref, f32[512,128]{1,0:T(8,128)S(1)} %get-tuple-element.8.y_ref, f32[6,192,1408]{2,1,0:T(8,128)S(1)} %get-tuple-element.9.m_ref), custom_call_target="tpu_custom_call" | custom-call | tf_op jit(solution)/shard_map/new_q_and_errors/pallas_call | solution.py:484

commit v4 on v3

--- a/solution.py
+++ b/solution.py
@@ -121,6 +121,12 @@
 
     near = tuple(over(link) for link in range(6))
     corner = tuple(over(link, (link + 1) % 6) for link in range(6))
+
+    def by_core(values):
+        first = core == 0
+        return tuple(
+            jax.tree.map(lambda a, b: jnp.where(first, a, b), values[i], values[(i + 3) % 6]) for i in range(6)
+        )
     sides = (side0(x), side0(y), side0(z), side1(x), side1(y), side1(z))
     twin = device(x, y, z, 1 - core)
     far = device(x, lax.rem(y + 2, 4), z, core)
@@ -223,41 +229,18 @@
 
         return 0
 
+    near_of, corner_of, side_of = by_core(near), by_core(corner), by_core(sides)
+
+    def three(src, dst, send, arrive, link):
+        targets = (near_of[(link + 1) % 6], near_of[link], corner_of[link])
+        return [remote(src(f), dst(f), send.at[f], arrive.at[f], targets[f]) for f in range(3)]
+
     halves = {}
-
-    def three(src, dst, send, arrive, link):
-        targets = (near[(link + 1) % 6], near[link], corner[link])
-        return [remote(src(f), dst.at[f], send.at[f], arrive.at[f], targets[f]) for f in range(3)]
-
-    def gram_chain(j):
-        halves[j] = hi, lo = split(p_out[j].T)
-        square = dot_nt(hi, hi) + (dot_nt(hi, lo) + dot_nt(lo, hi))
-        lane = lax.broadcasted_iota(jnp.int32, (R, 2 * R), 1)
-        gram_own[j] = jnp.where(lane < 64, square[:64], square[64:])
-        rows = pl.ds(pl.multiple_of(core * 32, 32), 32)
-        gram_half[j, 0] = gram_own[j, rows]
-        for s, link in enumerate((2, 5) if j % 2 == 0 else (5, 2)):
-            copies = three(
-                lambda f: gram_half.at[j, s], gram_recv.at[j, s], gram_send.at[j, s], gram_arrive.at[j, s], link,
-            )
-            yield
-            for copy in copies:
-                copy.wait()
-            got = gram_recv.at[j, s]
-            gram_half[j, s + 1] = (gram_half[j, s] + got[1]) + (got[0] + got[2])
-        copy = remote(
-            gram_half.at[j, 2], gram_recv.at[j, 2, 0], gram_send.at[j, 2, 0], gram_arrive.at[j, 2, 0], near[1],
-        )
-        yield
-        copy.wait()
-        gram_out[j, rows] = gram_half[j, 2] + gram_recv[j, 2, 0]
-        part = gram_out.at[j, rows]
-        copy = remote(part, part, gram_send.at[j, 2, 1], gram_arrive.at[j, 2, 1], twin)
-        yield
-        copy.wait()
 
     def local_g(m):
         j, b = divmod(m, 2)
+        if j not in halves:
+            halves[j] = split(p_out[j].T)
         hi, lo = halves[j]
         top = hi[64 * b : 64 * b + 64]
         both = jnp.concatenate([top, lo[64 * b : 64 * b + 64]], axis=0)
@@ -266,15 +249,41 @@
             wide = dot(both, mh[m, :, cols])
             g_acc[m, :, cols] = wide[:64] + wide[64:] + dot(top, ml[m, :, cols])
 
-    def g_chain(m):
-        link = [(m + s) % 6 for s in range(6)]
+    def gram_chain():
+        lane = lax.broadcasted_iota(jnp.int32, (R, 2 * R), 1)
+        for j in range(3):
+            hi, lo = halves[j]
+            square = dot_nt(hi, hi) + (dot_nt(hi, lo) + dot_nt(lo, hi))
+            gram_own[j] = jnp.where(lane < 64, square[:64], square[64:])
+        rows = pl.ds(pl.multiple_of(core * 32, 32), 32)
+        gram_half[0] = gram_own[:, rows]
+        for s, link in enumerate((2, 5)):
+            copies = three(
+                lambda f: gram_half.at[s], lambda f: gram_recv.at[s, f], gram_send.at[s], gram_arrive.at[s], link,
+            )
+            yield
+            for copy in copies:
+                copy.wait()
+            gram_half[s + 1] = (gram_half[s] + gram_recv[s, 1]) + (gram_recv[s, 0] + gram_recv[s, 2])
+        copy = remote(gram_half.at[2], gram_recv.at[2, 0], gram_send.at[2, 0], gram_arrive.at[2, 0], near[1])
+        yield
+        copy.wait()
+        gram_out[:, rows] = gram_half[2] + gram_recv[2, 0]
+        part = gram_out.at[:, rows]
+        copy = remote(part, part, gram_send.at[2, 1], gram_arrive.at[2, 1], twin)
+        yield
+        copy.wait()
+
+    def g_chain(j):
+        two = pl.ds(2 * j, 2)
+        link = [(2 * j + s) % 6 for s in range(6)]
         keep = pl.multiple_of(core * 32, 32)
         give = pl.multiple_of((1 - core) * 32, 32)
-        kept0 = pl.multiple_of(core * 32 + 16 * sides[link[0]], 16)
-        gone0 = pl.multiple_of(core * 32 + 16 - 16 * sides[link[0]], 16)
-        kept1 = pl.multiple_of(kept0 + 8 * sides[link[1]], 8)
-        gone1 = pl.multiple_of(kept0 + 8 - 8 * sides[link[1]], 8)
-        hi, lo = sides[link[2]], sides[link[3]]
+        kept0 = pl.multiple_of(core * 32 + 16 * side_of[link[0]], 16)
+        gone0 = pl.multiple_of(core * 32 + 16 - 16 * side_of[link[0]], 16)
+        kept1 = pl.multiple_of(kept0 + 8 * side_of[link[1]], 8)
+        gone1 = pl.multiple_of(kept0 + 8 - 8 * side_of[link[1]], 8)
+        hi, lo = side_of[link[2]], side_of[link[3]]
 
         def block(h, l):
             return pl.ds(pl.multiple_of((2 * h + l) * BLOCK, 128), BLOCK)
@@ -283,46 +292,49 @@
         others = (block(hi, 1 - lo), block(1 - hi, lo), block(1 - hi, 1 - lo))
 
         def send(s, src, dst, i):
-            return remote(src, dst, a_send.at[s, m], a_arrive.at[s, m], near[link[i]])
+            return remote(src, dst, a_send.at[s, j], a_arrive.at[s, j], near_of[link[i]])
 
         def forward(i, row, size):
-            part = g_sum.at[m, pl.ds(row, size), pl.ds(0, D)]
-            return remote(part, part, c_send.at[i, m], c_arrive.at[i, m], twin)
-
-        copy = remote(g_acc.at[m, pl.ds(give, 32)], core_recv.at[m], c_send.at[0, m], c_arrive.at[0, m], twin)
-        yield
-        copy.wait()
-        g_acc[m, pl.ds(keep, 32)] += core_recv[m]
-        copy = send(0, g_acc.at[m, pl.ds(gone0, 16)], recv0.at[m], 0)
-        yield
-        copy.wait()
-        g_acc[m, pl.ds(kept0, 16)] += recv0[m]
-        copy = send(1, g_acc.at[m, pl.ds(gone1, 8)], recv1.at[m], 1)
-        yield
-        copy.wait()
-        q_acc[m, :, :D] = g_acc[m, pl.ds(kept1, 8)] + recv1[m]
-        copies = three(lambda f: q_acc.at[m, :, others[f]], recv2.at[m], b_send.at[0, m], b_arrive.at[0, m], link[2])
+            part = g_sum.at[two, pl.ds(row, size), pl.ds(0, D)]
+            return remote(part, part, c_send.at[i, j], c_arrive.at[i, j], twin)
+
+        copy = remote(g_acc.at[two, pl.ds(give, 32)], core_recv.at[two], c_send.at[0, j], c_arrive.at[0, j], twin)
+        yield
+        copy.wait()
+        g_acc[two, pl.ds(keep, 32)] += core_recv[two]
+        copy = send(0, g_acc.at[two, pl.ds(gone0, 16)], recv0.at[two], 0)
+        yield
+        copy.wait()
+        g_acc[two, pl.ds(kept0, 16)] += recv0[two]
+        copy = send(1, g_acc.at[two, pl.ds(gone1, 8)], recv1.at[two], 1)
+        yield
+        copy.wait()
+        q_acc[two, :, :D] = g_acc[two, pl.ds(kept1, 8)] + recv1[two]
+        copies = three(
+            lambda f: q_acc.at[two, :, others[f]], lambda f: recv2.at[f, two], b_send.at[0, j], b_arrive.at[0, j], link[2],
+        )
         yield
         for copy in copies:
             copy.wait()
-        x_acc[m] = (q_acc[m, :, own] + recv2[m, 1]) + (recv2[m, 0] + recv2[m, 2])
-        copies = three(lambda f: x_acc.at[m], recv3.at[m], b_send.at[1, m], b_arrive.at[1, m], link[4])
+        x_acc[two] = (q_acc[two, :, own] + recv2[1, two]) + (recv2[0, two] + recv2[2, two])
+        copies = three(
+            lambda f: x_acc.at[two], lambda f: recv3.at[f, two], b_send.at[1, j], b_arrive.at[1, j], link[4],
+        )
         yield
         for copy in copies:
             copy.wait()
-        g_sum[m, pl.ds(kept1, 8), own] = (x_acc[m] + recv3[m, 1]) + (recv3[m, 0] + recv3[m, 2])
-        part = g_sum.at[m, pl.ds(kept1, 8), own]
-        targets = (near[link[3]], near[link[2]], corner[link[2]])
-        copies = [remote(part, part, b_send.at[2, m, f], b_arrive.at[2, m, f], targets[f]) for f in range(3)]
+        g_sum[two, pl.ds(kept1, 8), own] = (x_acc[two] + recv3[1, two]) + (recv3[0, two] + recv3[2, two])
+        part = g_sum.at[two, pl.ds(kept1, 8), own]
+        copies = three(lambda f: part, lambda f: part, b_send.at[2, j], b_arrive.at[2, j], link[2])
         yield
         for copy in copies:
             copy.wait()
-        part = g_sum.at[m, pl.ds(kept1, 8), pl.ds(0, D)]
+        part = g_sum.at[two, pl.ds(kept1, 8), pl.ds(0, D)]
         copy = send(2, part, part, 1)
         passed = [forward(1, kept1, 8)]
         yield
         copy.wait()
-        part = g_sum.at[m, pl.ds(kept0, 16), pl.ds(0, D)]
+        part = g_sum.at[two, pl.ds(kept0, 16), pl.ds(0, D)]
         copy = send(3, part, part, 0)
         passed.append(forward(2, gone1, 8))
         yield
@@ -332,57 +344,46 @@
         for copy in passed:
             copy.wait()
 
-    gc = [gram_chain(j) for j in range(3)]
-    ac = [g_chain(m) for m in range(MATS)]
+    gram = gram_chain()
+    ac = [g_chain(j) for j in range(3)]
     factor = None
 
-    def behind():
+    def behind(blocks):
         nonlocal factor
-        if factor is None:
-            if all([next(chain, 1) for chain in gc]):
-                factor = eliminate([gram_out[j] for j in range(3)], y_out)
+        if factor is None and next(gram, 1):
+            factor = eliminate([gram_out[j] for j in range(3)], y_out)
         if factor is not None:
-            next(factor, None)
+            for _ in range(blocks):
+                next(factor, None)
 
     lax.fori_loop(0, MATS, p_loop, 0)
     p_step(1, 2)
     p_step(3, 0)
-    next(gc[0])
     local_g(0)
-    next(ac[0])
     p_step(2, 1)
     local_g(1)
-    next(ac[1])
+    next(ac[0])
     p_step(2, 2)
     p_step(3, 1)
-    next(gc[1])
-    next(gc[0])
     local_g(2)
+    local_g(3)
+    next(ac[1])
+    next(ac[0])
+    p_step(3, 2)
+    halves[2] = split(p_out[2].T)
+    next(gram)
+    local_g(4)
+    local_g(5)
     next(ac[2])
+    next(ac[1])
+    behind(0)
     next(ac[0])
-    local_g(3)
-    next(ac[3])
-    next(ac[1])
-    p_step(3, 2)
-    next(gc[2])
-    next(gc[1])
-    next(gc[0])
-    local_g(4)
-    next(ac[4])
     next(ac[2])
-    local_g(5)
-    next(ac[5])
-    next(ac[3])
-    next(gc[2])
-    next(gc[1])
-    next(gc[0])
-    next(ac[4])
-    next(ac[5])
     for s in range(8):
-        for m in range(MATS):
-            next(ac[m], None)
-            if factor is not None or m in (2, 5):
-                behind()
+        for j in range(3):
+            next(ac[j], None)
+            if factor is not None or j != 1:
+                behind(2)
     for _ in factor:
         pass
 
@@ -458,23 +459,23 @@
             pltpu.VMEM((MATS, 8, D), f32),
             pltpu.VMEM((MATS, 8, 4 * BLOCK), f32),
             pltpu.VMEM((MATS, 8, BLOCK), f32),
-            pltpu.VMEM((MATS, 3, 8, BLOCK), f32),
-            pltpu.VMEM((MATS, 3, 8, BLOCK), f32),
+            pltpu.VMEM((3, MATS, 8, BLOCK), f32),
+            pltpu.VMEM((3, MATS, 8, BLOCK), f32),
             pltpu.VMEM((MATS // 2, R, 2 * R), f32),
-            pltpu.VMEM((MATS // 2, 3, R // 2, 2 * R), f32),
-            pltpu.VMEM((MATS // 2, 3, 3, R // 2, 2 * R), f32),
+            pltpu.VMEM((3, MATS // 2, R // 2, 2 * R), f32),
+            pltpu.VMEM((3, 3, MATS // 2, R // 2, 2 * R), f32),
             pltpu.VMEM((MATS // 2, R, 2 * R), f32),
             sem((MATS, 3)),
             sem((3, 3)),
             sem((3, 3)),
-            sem((4, MATS)),
-            sem((4, MATS)),
-            sem((4, MATS)),
-            sem((4, MATS)),
-            sem((3, MATS, 3)),
-            sem((3, MATS, 3)),
+            sem((4, 3)),
+            sem((4, 3)),
+            sem((4, 3)),
+            sem((4, 3)),
             sem((3, 3, 3)),
             sem((3, 3, 3)),
+            sem((3, 3)),
+            sem((3, 3)),
         ],
         compiler_params=pltpu.CompilerParams(
             collective_id=0, has_side_effects=True, vmem_limit_bytes=40 * 2**20

time: 62.8 us -> 64.3 us (1.024)
  Pallas kernels: 62.1 us -> 63.5 us
    pallas_call x1, Pallas kernels: 58 us -> 59.5 us  [body(): pl.pallas_call(comm_kernel, out_shape=(jax.ShapeDtypeStruct((MATS, R, 4 *...]
where the time goes in v4:
time: 64.3 us; the launch traced here: 64.2 us
  Pallas kernels  63.5 us (99%)
    pallas_call x1, Pallas kernels, body(): pl.pallas_call(comm_kernel, out_shape=(jax.ShapeDtypeStruct((MATS, R, 4 *...  59.5 us
    pallas_call x1, Pallas kernels, body(): pl.pallas_call(finish_kernel, out_shape=(jax.ShapeDtypeStruct((1, MATS, R...  4.04 us

profile of v4, /device:TPU:1, one launch (start us, length us, event | category | flops | bytes accessed | tf_op | source)
XLA Modules:
  0.0 64.2 jit_solution(12647861472983852334)
XLA Ops:
  0.6 59.5 %compress_and_sum.1 = (f32[6,64,1536]{2,1,0:T(8,128)S(1)}, f32[3,192,128]{2,1,0:T(8,128)S(1)}, f32[512,128]{1,0:T(8,128)S(1)}, f32[6,192,1408]{2,1,0:T(8,128)S(1)}) custom-call(bf16[1,6,192,1408]{3,2,1,0:T(8,128)(2,1)} %g_hbm.1, f32[1,6,192,1408]{3,2,1,0:T(8,128)} %e_hbm.1, f32[6,64,1408]{2,1,0:T(8,128)} %q_hbm.1), custom_call_target="tpu_custom_call" | custom-call | tf_op jit(solution)/shard_map/compress_and_sum/pallas_call | solution.py:436
  60.1 4.0 %new_q_and_errors.1 = (f32[1,6,192,1408]{3,2,1,0:T(8,128)}, f32[6,64,1408]{2,1,0:T(8,128)}) custom-call(f32[6,64,1536]{2,1,0:T(8,128)S(1)} %get-tuple-element.6.g_sum, f32[3,192,128]{2,1,0:T(8,128)S(1)} %get-tuple-element.7.p_ref, f32[512,128]{1,0:T(8,128)S(1)} %get-tuple-element.8.y_ref, f32[6,192,1408]{2,1,0:T(8,128)S(1)} %get-tuple-element.9.m_ref), custom_call_target="tpu_custom_call" | custom-call | tf_op jit(solution)/shard_map/new_q_and_errors/pallas_call | solution.py:485

commit v5 on v3

--- a/solution.py
+++ b/solution.py
@@ -81,11 +81,57 @@
         yield
 
 
+def product_kernel(g_hbm, e_hbm, q_hbm, ebuf, mh, ml, p_own, gbuf, qbuf, qst, load_sem):
+    def loads(m):
+        return (
+            pltpu.make_async_copy(q_hbm.at[m], qbuf.at[m], load_sem.at[m, 0]),
+            pltpu.make_async_copy(g_hbm.at[0, m], gbuf.at[m], load_sem.at[m, 1]),
+            pltpu.make_async_copy(e_hbm.at[0, m], ebuf.at[m], load_sem.at[m, 2]),
+        )
+
+    def begin(m, _):
+        for copy in loads(m):
+            copy.start()
+        return 0
+
+    lax.fori_loop(0, MATS, begin, 0)
+    p_own[...] = jnp.zeros_like(p_own)
+    qst[...] = jnp.zeros_like(qst)
+
+    def local_p(m):
+        b = lax.rem(m, 2)
+        for copy in loads(m):
+            copy.wait()
+
+        def merge(i, _):
+            rows = pl.ds(pl.multiple_of(i * 32, 32), 32)
+            merged = gbuf[m, rows].astype(f32) + ebuf[m, rows]
+            ebuf[m, rows] = merged
+            hi, lo = split(merged)
+            mh[m, rows] = hi
+            ml[m, rows] = lo
+            return 0
+
+        lax.fori_loop(0, ROWS // 32, merge, 0)
+        hi, lo = split(qbuf[m])
+        at = pl.multiple_of(64 * b, 64)
+        qst[b, pl.ds(at, 64)] = hi
+        qst[b, pl.ds(at + 128, 64)] = lo
+        wide = dot_nt(mh[m], qst[b])
+        p_own[lax.div(m, 2)] += wide[:, :128] + wide[:, 128:] + dot_nt(ml[m], qst[b, :128])
+
+    def p_loop(m, _):
+        local_p(m)
+        return 0
+
+    lax.fori_loop(0, MATS, p_loop, 0)
+
+
 def comm_kernel(
-    g_hbm, e_hbm, q_hbm, g_sum, p_out, y_out, ebuf,
-    gbuf, qbuf, mh, ml, qst, p_own, p_recv, p_chip, p_far, g_acc,
+    mh, ml, p_own, g_sum, p_out, y_out,
+    p_recv, p_chip, p_far, g_acc,
     core_recv, recv0, recv1, q_acc, x_acc, recv2, recv3, gram_own, gram_half, gram_recv, gram_out,
-    load_sem, p_send, p_arrive, c_send, c_arrive, a_send, a_arrive, b_send, b_arrive,
+    p_send, p_arrive, c_send, c_arrive, a_send, a_arrive, b_send, b_arrive,
     gram_send, gram_arrive,
 ):
     dp, mp = lax.axis_index("dp"), lax.axis_index("mp")
@@ -125,19 +171,6 @@
     twin = device(x, y, z, 1 - core)
     far = device(x, lax.rem(y + 2, 4), z, core)
 
-    def loads(m):
-        return (
-            pltpu.make_async_copy(q_hbm.at[m], qbuf.at[m], load_sem.at[m, 0]),
-            pltpu.make_async_copy(g_hbm.at[0, m], gbuf.at[m], load_sem.at[m, 1]),
-            pltpu.make_async_copy(e_hbm.at[0, m], ebuf.at[m], load_sem.at[m, 2]),
-        )
-
-    def begin(m, _):
-        for copy in loads(m):
-            copy.start()
-        return 0
-
-    lax.fori_loop(0, MATS, begin, 0)
     barrier = pltpu.get_barrier_semaphore()
     everyone = near + corner + (twin, far)
     for other in everyone:
@@ -153,31 +186,7 @@
 
     mine = pl.multiple_of(core * HALF, 8)
     theirs = pl.multiple_of((1 - core) * HALF, 8)
-    p_own[...] = jnp.zeros_like(p_own)
-    qst[...] = jnp.zeros_like(qst)
     q_acc[...] = jnp.zeros_like(q_acc)
-
-    def local_p(m):
-        b = lax.rem(m, 2)
-        for copy in loads(m):
-            copy.wait()
-
-        def merge(i, _):
-            rows = pl.ds(pl.multiple_of(i * 32, 32), 32)
-            merged = gbuf[m, rows].astype(f32) + ebuf[m, rows]
-            ebuf[m, rows] = merged
-            hi, lo = split(merged)
-            mh[m, rows] = hi
-            ml[m, rows] = lo
-            return 0
-
-        lax.fori_loop(0, ROWS // 32, merge, 0)
-        hi, lo = split(qbuf[m])
-        at = pl.multiple_of(64 * b, 64)
-        qst[b, pl.ds(at, 64)] = hi
-        qst[b, pl.ds(at + 128, 64)] = lo
-        wide = dot_nt(mh[m], qst[b])
-        p_own[lax.div(m, 2)] += wide[:, :128] + wide[:, 128:] + dot_nt(ml[m], qst[b, :128])
 
     def p_copy(s, j):
         if s == 0:
@@ -201,27 +210,6 @@
             p_out[j, pl.ds(mine, HALF)] = (p_chip[j] + p_far[j]) * 0.25
         if s < 3:
             p_copy(s, j).start()
-
-    def p_loop(m, _):
-        local_p(m)
-
-        @pl.when(m == 1)
-        def _():
-            pl.semaphore_wait(barrier, len(everyone))
-            p_step(0, 0)
-
-        @pl.when(m == 3)
-        def _():
-            p_step(0, 1)
-            p_step(1, 0)
-
-        @pl.when(m == 5)
-        def _():
-            p_step(0, 2)
-            p_step(1, 1)
-            p_step(2, 0)
-
-        return 0
 
     halves = {}
 
@@ -344,16 +332,16 @@
         if factor is not None:
             next(factor, None)
 
-    lax.fori_loop(0, MATS, p_loop, 0)
-    p_step(1, 2)
+    pl.semaphore_wait(barrier, len(everyone))
+    for i in range(3):
+        for j in range(3):
+            p_step(i, j)
     p_step(3, 0)
     next(gc[0])
     local_g(0)
     next(ac[0])
-    p_step(2, 1)
     local_g(1)
     next(ac[1])
-    p_step(2, 2)
     p_step(3, 1)
     next(gc[1])
     next(gc[0])
@@ -432,23 +420,36 @@
     vmem = pl.BlockSpec(memory_space=pltpu.VMEM)
     far_hbm = pl.BlockSpec(memory_space=pltpu.HBM)
     sem = pltpu.SemaphoreType.DMA
-    g_sum, p_mat, y_mat, merged = pl.pallas_call(
+    from_hbm = [pltpu.with_memory_space_constraint(v, pltpu.HBM) for v in (gradients, errors, previous_q)]
+    merged, high, low, p_own = pl.pallas_call(
+        product_kernel,
+        out_shape=(
+            jax.ShapeDtypeStruct((MATS, ROWS, D), f32),
+            jax.ShapeDtypeStruct((MATS, ROWS, D), bf16),
+            jax.ShapeDtypeStruct((MATS, ROWS, D), bf16),
+            jax.ShapeDtypeStruct((MATS // 2, ROWS, 128), f32),
+        ),
+        in_specs=[far_hbm] * 3,
+        out_specs=(vmem,) * 4,
+        scratch_shapes=[
+            pltpu.VMEM((MATS, ROWS, D), bf16),
+            pltpu.VMEM((MATS, R, D), f32),
+            pltpu.VMEM((2, 256, D), bf16),
+            sem((MATS, 3)),
+        ],
+        compiler_params=pltpu.CompilerParams(vmem_limit_bytes=30 * 2**20),
+        name="merge_and_product",
+    )(*from_hbm)
+    g_sum, p_mat, y_mat = pl.pallas_call(
         comm_kernel,
         out_shape=(
             jax.ShapeDtypeStruct((MATS, R, 4 * BLOCK), f32),
             jax.ShapeDtypeStruct((MATS // 2, ROWS, 2 * R), f32),
             jax.ShapeDtypeStruct((8 * R, 2 * R), f32),
-            jax.ShapeDtypeStruct((MATS, ROWS, D), f32),
         ),
-        in_specs=[far_hbm, far_hbm, far_hbm],
-        out_specs=(vmem, vmem, vmem, vmem),
+        in_specs=[vmem] * 3,
+        out_specs=(vmem,) * 3,
         scratch_shapes=[
-            pltpu.VMEM((MATS, ROWS, D), bf16),
-            pltpu.VMEM((MATS, R, D), f32),
-            pltpu.VMEM((MATS, ROWS, D), bf16),
-            pltpu.VMEM((MATS, ROWS, D), bf16),
-            pltpu.VMEM((2, 256, D), bf16),
-            pltpu.VMEM((MATS // 2, ROWS, 128), f32),
             pltpu.VMEM((MATS // 2, HALF, 128), f32),
             pltpu.VMEM((MATS // 2, HALF, 128), f32),
             pltpu.VMEM((MATS // 2, HALF, 128), f32),
@@ -464,7 +465,6 @@
             pltpu.VMEM((MATS // 2, 3, R // 2, 2 * R), f32),
             pltpu.VMEM((MATS // 2, 3, 3, R // 2, 2 * R), f32),
             pltpu.VMEM((MATS // 2, R, 2 * R), f32),
-            sem((MATS, 3)),
             sem((3, 3)),
             sem((3, 3)),
             sem((4, MATS)),
@@ -477,10 +477,10 @@
             sem((3, 3, 3)),
         ],
         compiler_params=pltpu.CompilerParams(
-            collective_id=0, has_side_effects=True, vmem_limit_bytes=40 * 2**20
+            collective_id=0, has_side_effects=True, vmem_limit_bytes=30 * 2**20
         ),
-        name="compress_and_sum",
-    )(*[pltpu.with_memory_space_constraint(v, pltpu.HBM) for v in (gradients, errors, previous_q)])
+        name="exchange_and_sum",
+    )(high, low, p_own)
     return pl.pallas_call(
         finish_kernel,
         out_shape=(

time: 62.8 us -> 68.5 us (1.091)
  Pallas kernels: 62.1 us -> 67.7 us
    pallas_call x0 -> x1, Pallas kernels: none -> 6.95 us  [body(): pl.pallas_call(product_kernel, out_shape=(jax.ShapeDtypeStruct((MATS, ROW...]
    pallas_call x1, Pallas kernels: 58 us -> 56.7 us  [body(): pl.pallas_call(comm_kernel, out_shape=(jax.ShapeDtypeStruct((MATS, R, 4 *...]
where the time goes in v5:
time: 68.5 us; the launch traced here: 68.4 us
  Pallas kernels  67.7 us (99%)
    pallas_call x1, Pallas kernels, body(): pl.pallas_call(comm_kernel, out_shape=(jax.ShapeDtypeStruct((MATS, R, 4 *...  56.7 us
    pallas_call x1, Pallas kernels, body(): pl.pallas_call(product_kernel, out_shape=(jax.ShapeDtypeStruct((MATS, ROW...  6.95 us
    pallas_call x1, Pallas kernels, body(): pl.pallas_call(finish_kernel, out_shape=(jax.ShapeDtypeStruct((1, MATS, R...  4.05 us

profile of v5, /device:TPU:1, one launch (start us, length us, event | category | flops | bytes accessed | tf_op | source)
XLA Modules:
  0.0 68.4 jit_solution(2486565894631645271)
XLA Ops:
  0.6 7.0 %merge_and_product.1 = (f32[6,192,1408]{2,1,0:T(8,128)S(1)}, bf16[6,192,1408]{2,1,0:T(8,128)(2,1)S(1)}, bf16[6,192,1408]{2,1,0:T(8,128)(2,1)S(1)}, f32[3,192,128]{2,1,0:T(8,128)S(1)}) custom-call(bf16[1,6,192,1408]{3,2,1,0:T(8,128)(2,1)} %g_hbm.1, f32[1,6,192,1408]{3,2,1,0:T(8,128)} %e_hbm.1, f32[6,64,1408]{2,1,0:T(8,128)} %q_hbm.1), custom_call_target="tpu_custom_call" | custom-call | tf_op jit(solution)/shard_map/merge_and_product/pallas_call | solution.py:424
  7.6 56.7 %exchange_and_sum.1 = (f32[6,64,1536]{2,1,0:T(8,128)S(1)}, f32[3,192,128]{2,1,0:T(8,128)S(1)}, f32[512,128]{1,0:T(8,128)S(1)}) custom-call(bf16[6,192,1408]{2,1,0:T(8,128)(2,1)S(1)} %get-tuple-element.9.mh, bf16[6,192,1408]{2,1,0:T(8,128)(2,1)S(1)} %get-tuple-element.10.ml, f32[3,192,128]{2,1,0:T(8,128)S(1)} %get-tuple-element.11.p_own), custom_call_target="tpu_custom_call" | custom-call | tf_op jit(solution)/shard_map/exchange_and_sum/pallas_call | solution.py:443
  64.3 4.0 %new_q_and_errors.1 = (f32[1,6,192,1408]{3,2,1,0:T(8,128)}, f32[6,64,1408]{2,1,0:T(8,128)}) custom-call(f32[6,64,1536]{2,1,0:T(8,128)S(1)} %get-tuple-element.12.g_sum, f32[3,192,128]{2,1,0:T(8,128)S(1)} %get-tuple-element.13.p_ref, f32[512,128]{1,0:T(8,128)S(1)} %get-tuple-element.14.y_ref, f32[6,192,1408]{2,1,0:T(8,128)S(1)} %get-tuple-element.15.m_ref), custom_call_target="tpu_custom_call" | custom-call | tf_op jit(solution)/shard_map/new_q_and_errors/pallas_call | solution.py:484

commit v6 on v3

--- a/solution.py
+++ b/solution.py
@@ -282,24 +282,37 @@
         own = block(hi, lo)
         others = (block(hi, 1 - lo), block(1 - hi, lo), block(1 - hi, 1 - lo))
 
-        def send(s, src, dst, i):
-            return remote(src, dst, a_send.at[s, m], a_arrive.at[s, m], near[link[i]])
+        def pieces(src, first, dst, place, size, send, arrive, target):
+            return [
+                remote(
+                    src.at[m, pl.ds(pl.multiple_of(first + r, 8), 8), pl.ds(0, D)],
+                    dst.at[m, pl.ds(pl.multiple_of(place + r, 8), 8), pl.ds(0, D)],
+                    send.at[m, r // 8], arrive.at[m, r // 8], target,
+                )
+                for r in range(0, size, 8)
+            ]
+
+        def send(s, src, first, dst, place, size, i):
+            return pieces(src, first, dst, place, size, a_send.at[s], a_arrive.at[s], near[link[i]])
 
         def forward(i, row, size):
-            part = g_sum.at[m, pl.ds(row, size), pl.ds(0, D)]
-            return remote(part, part, c_send.at[i, m], c_arrive.at[i, m], twin)
-
-        copy = remote(g_acc.at[m, pl.ds(give, 32)], core_recv.at[m], c_send.at[0, m], c_arrive.at[0, m], twin)
-        yield
-        copy.wait()
+            return pieces(g_sum, row, g_sum, row, size, c_send.at[i], c_arrive.at[i], twin)
+
+        def wait(copies):
+            for copy in copies:
+                copy.wait()
+
+        copy = pieces(g_acc, give, core_recv, 0, 32, c_send.at[0], c_arrive.at[0], twin)
+        yield
+        wait(copy)
         g_acc[m, pl.ds(keep, 32)] += core_recv[m]
-        copy = send(0, g_acc.at[m, pl.ds(gone0, 16)], recv0.at[m], 0)
-        yield
-        copy.wait()
+        copy = send(0, g_acc, gone0, recv0, 0, 16, 0)
+        yield
+        wait(copy)
         g_acc[m, pl.ds(kept0, 16)] += recv0[m]
-        copy = send(1, g_acc.at[m, pl.ds(gone1, 8)], recv1.at[m], 1)
-        yield
-        copy.wait()
+        copy = send(1, g_acc, gone1, recv1, 0, 8, 1)
+        yield
+        wait(copy)
         q_acc[m, :, :D] = g_acc[m, pl.ds(kept1, 8)] + recv1[m]
         copies = three(lambda f: q_acc.at[m, :, others[f]], recv2.at[m], b_send.at[0, m], b_arrive.at[0, m], link[2])
         yield
@@ -317,20 +330,18 @@
         yield
         for copy in copies:
             copy.wait()
-        part = g_sum.at[m, pl.ds(kept1, 8), pl.ds(0, D)]
-        copy = send(2, part, part, 1)
+        copy = send(2, g_sum, kept1, g_sum, kept1, 8, 1)
         passed = [forward(1, kept1, 8)]
         yield
-        copy.wait()
-        part = g_sum.at[m, pl.ds(kept0, 16), pl.ds(0, D)]
-        copy = send(3, part, part, 0)
+        wait(copy)
+        copy = send(3, g_sum, kept0, g_sum, kept0, 16, 0)
         passed.append(forward(2, gone1, 8))
         yield
-        copy.wait()
+        wait(copy)
         passed.append(forward(3, gone0, 16))
         yield
         for copy in passed:
-            copy.wait()
+            wait(copy)
 
     gc = [gram_chain(j) for j in range(3)]
     ac = [g_chain(m) for m in range(MATS)]
@@ -467,10 +478,10 @@
             sem((MATS, 3)),
             sem((3, 3)),
             sem((3, 3)),
-            sem((4, MATS)),
-            sem((4, MATS)),
-            sem((4, MATS)),
-            sem((4, MATS)),
+            sem((4, MATS, 4)),
+            sem((4, MATS, 4)),
+            sem((4, MATS, 2)),
+            sem((4, MATS, 2)),
             sem((3, MATS, 3)),
             sem((3, MATS, 3)),
             sem((3, 3, 3)),

time: 62.8 us -> 64.6 us (1.029)
  Pallas kernels: 62.1 us -> 63.8 us
    pallas_call x1, Pallas kernels: 58 us -> 59.8 us  [body(): pl.pallas_call(comm_kernel, out_shape=(jax.ShapeDtypeStruct((MATS, R, 4 *...]
where the time goes in v6:
time: 64.6 us; the launch traced here: 64.5 us
  Pallas kernels  63.8 us (99%)
    pallas_call x1, Pallas kernels, body(): pl.pallas_call(comm_kernel, out_shape=(jax.ShapeDtypeStruct((MATS, R, 4 *...  59.8 us
    pallas_call x1, Pallas kernels, body(): pl.pallas_call(finish_kernel, out_shape=(jax.ShapeDtypeStruct((1, MATS, R...  4.05 us

profile of v6, /device:TPU:1, one launch (start us, length us, event | category | flops | bytes accessed | tf_op | source)
XLA Modules:
  0.0 64.5 jit_solution(4736039279996728590)
XLA Ops:
  0.6 59.8 %compress_and_sum.1 = (f32[6,64,1536]{2,1,0:T(8,128)S(1)}, f32[3,192,128]{2,1,0:T(8,128)S(1)}, f32[512,128]{1,0:T(8,128)S(1)}, f32[6,192,1408]{2,1,0:T(8,128)S(1)}) custom-call(bf16[1,6,192,1408]{3,2,1,0:T(8,128)(2,1)} %g_hbm.1, f32[1,6,192,1408]{3,2,1,0:T(8,128)} %e_hbm.1, f32[6,64,1408]{2,1,0:T(8,128)} %q_hbm.1), custom_call_target="tpu_custom_call" | custom-call | tf_op jit(solution)/shard_map/compress_and_sum/pallas_call | solution.py:446
  60.4 4.0 %new_q_and_errors.1 = (f32[1,6,192,1408]{3,2,1,0:T(8,128)}, f32[6,64,1408]{2,1,0:T(8,128)}) custom-call(f32[6,64,1536]{2,1,0:T(8,128)S(1)} %get-tuple-element.6.g_sum, f32[3,192,128]{2,1,0:T(8,128)S(1)} %get-tuple-element.7.p_ref, f32[512,128]{1,0:T(8,128)S(1)} %get-tuple-element.8.y_ref, f32[6,192,1408]{2,1,0:T(8,128)S(1)} %get-tuple-element.9.m_ref), custom_call_target="tpu_custom_call" | custom-call | tf_op jit(solution)/shard_map/new_q_and_errors/pallas_call | solution.py:495

commit v7 on v3

--- a/solution.py
+++ b/solution.py
@@ -143,12 +143,15 @@
     for other in everyone:
         pl.semaphore_signal(barrier, inc=1, device_id=other, device_id_type=MESH)
 
+    sent = []
+
     def remote(src, dst, send, arrive, target):
         copy = pltpu.make_async_remote_copy(
             src_ref=src, dst_ref=dst, send_sem=send, recv_sem=arrive,
             device_id=target, device_id_type=MESH,
         )
         copy.start()
+        sent.append(copy)
         return copy
 
     mine = pl.multiple_of(core * HALF, 8)
@@ -194,7 +197,7 @@
 
     def p_step(s, j):
         if s > 0:
-            p_copy(s - 1, j).wait()
+            p_copy(s - 1, j).wait_recv()
         if s == 1:
             p_chip[j] = p_own[j, pl.ds(mine, HALF)] + p_recv[j]
         if s == 2:
@@ -242,19 +245,19 @@
             )
             yield
             for copy in copies:
-                copy.wait()
+                copy.wait_recv()
             got = gram_recv.at[j, s]
             gram_half[j, s + 1] = (gram_half[j, s] + got[1]) + (got[0] + got[2])
         copy = remote(
             gram_half.at[j, 2], gram_recv.at[j, 2, 0], gram_send.at[j, 2, 0], gram_arrive.at[j, 2, 0], near[1],
         )
         yield
-        copy.wait()
+        copy.wait_recv()
         gram_out[j, rows] = gram_half[j, 2] + gram_recv[j, 2, 0]
         part = gram_out.at[j, rows]
         copy = remote(part, part, gram_send.at[j, 2, 1], gram_arrive.at[j, 2, 1], twin)
         yield
-        copy.wait()
+        copy.wait_recv()
 
     def local_g(m):
         j, b = divmod(m, 2)
@@ -291,46 +294,46 @@
 
         copy = remote(g_acc.at[m, pl.ds(give, 32)], core_recv.at[m], c_send.at[0, m], c_arrive.at[0, m], twin)
         yield
-        copy.wait()
+        copy.wait_recv()
         g_acc[m, pl.ds(keep, 32)] += core_recv[m]
         copy = send(0, g_acc.at[m, pl.ds(gone0, 16)], recv0.at[m], 0)
         yield
-        copy.wait()
+        copy.wait_recv()
         g_acc[m, pl.ds(kept0, 16)] += recv0[m]
         copy = send(1, g_acc.at[m, pl.ds(gone1, 8)], recv1.at[m], 1)
         yield
-        copy.wait()
+        copy.wait_recv()
         q_acc[m, :, :D] = g_acc[m, pl.ds(kept1, 8)] + recv1[m]
         copies = three(lambda f: q_acc.at[m, :, others[f]], recv2.at[m], b_send.at[0, m], b_arrive.at[0, m], link[2])
         yield
         for copy in copies:
-            copy.wait()
+            copy.wait_recv()
         x_acc[m] = (q_acc[m, :, own] + recv2[m, 1]) + (recv2[m, 0] + recv2[m, 2])
         copies = three(lambda f: x_acc.at[m], recv3.at[m], b_send.at[1, m], b_arrive.at[1, m], link[4])
         yield
         for copy in copies:
-            copy.wait()
+            copy.wait_recv()
         g_sum[m, pl.ds(kept1, 8), own] = (x_acc[m] + recv3[m, 1]) + (recv3[m, 0] + recv3[m, 2])
         part = g_sum.at[m, pl.ds(kept1, 8), own]
         targets = (near[link[3]], near[link[2]], corner[link[2]])
         copies = [remote(part, part, b_send.at[2, m, f], b_arrive.at[2, m, f], targets[f]) for f in range(3)]
         yield
         for copy in copies:
-            copy.wait()
+            copy.wait_recv()
         part = g_sum.at[m, pl.ds(kept1, 8), pl.ds(0, D)]
         copy = send(2, part, part, 1)
         passed = [forward(1, kept1, 8)]
         yield
-        copy.wait()
+        copy.wait_recv()
         part = g_sum.at[m, pl.ds(kept0, 16), pl.ds(0, D)]
         copy = send(3, part, part, 0)
         passed.append(forward(2, gone1, 8))
         yield
-        copy.wait()
+        copy.wait_recv()
         passed.append(forward(3, gone0, 16))
         yield
         for copy in passed:
-            copy.wait()
+            copy.wait_recv()
 
     gc = [gram_chain(j) for j in range(3)]
     ac = [g_chain(m) for m in range(MATS)]
@@ -385,6 +388,11 @@
                 behind()
     for _ in factor:
         pass
+    for s in range(3):
+        for j in range(3):
+            p_copy(s, j).wait_send()
+    for copy in sent:
+        copy.wait_send()
 
 
 def finish_kernel(

time: 62.8 us -> 63.1 us (level)
  no operation moved by 1% of the time
where the time goes in v7:
time: 63.1 us; the launch traced here: 63 us
  Pallas kernels  62.3 us (99%)
  between operations  0.64 us (1%)
    pallas_call x1, Pallas kernels, body(): pl.pallas_call(comm_kernel, out_shape=(jax.ShapeDtypeStruct((MATS, R, 4 *...  58.3 us
    pallas_call x1, Pallas kernels, body(): pl.pallas_call(finish_kernel, out_shape=(jax.ShapeDtypeStruct((1, MATS, R...  4.04 us

profile of v7, /device:TPU:1, one launch (start us, length us, event | category | flops | bytes accessed | tf_op | source)
XLA Modules:
  0.0 63.0 jit_solution(3913001814219763991)
XLA Ops:
  0.6 58.3 %compress_and_sum.1 = (f32[6,64,1536]{2,1,0:T(8,128)S(1)}, f32[3,192,128]{2,1,0:T(8,128)S(1)}, f32[512,128]{1,0:T(8,128)S(1)}, f32[6,192,1408]{2,1,0:T(8,128)S(1)}) custom-call(bf16[1,6,192,1408]{3,2,1,0:T(8,128)(2,1)} %g_hbm.1, f32[1,6,192,1408]{3,2,1,0:T(8,128)} %e_hbm.1, f32[6,64,1408]{2,1,0:T(8,128)} %q_hbm.1), custom_call_target="tpu_custom_call" | custom-call | tf_op jit(solution)/shard_map/compress_and_sum/pallas_call | solution.py:443
  58.9 4.0 %new_q_and_errors.1 = (f32[1,6,192,1408]{3,2,1,0:T(8,128)}, f32[6,64,1408]{2,1,0:T(8,128)}) custom-call(f32[6,64,1536]{2,1,0:T(8,128)S(1)} %get-tuple-element.6.g_sum, f32[3,192,128]{2,1,0:T(8,128)S(1)} %get-tuple-element.7.p_ref, f32[512,128]{1,0:T(8,128)S(1)} %get-tuple-element.8.y_ref, f32[6,192,1408]{2,1,0:T(8,128)S(1)} %get-tuple-element.9.m_ref), custom_call_target="tpu_custom_call" | custom-call | tf_op jit(solution)/shard_map/new_q_and_errors/pallas_call | solution.py:492

commit v8 on v7

--- a/solution.py
+++ b/solution.py
@@ -13,6 +13,23 @@
 BLOCK = 384
 COLS = ((0, 512), (512, 512), (1024, 384))
 f32, bf16 = jnp.float32, jnp.bfloat16
+FIRST_LINK = (0, 3, 2, 5, 1, 4)
+ORDER = (
+    ("products", 0), ("p", 0), ("products", 1), ("p", 1), ("p", 0), ("products", 2), ("p", 2), ("p", 1),
+    ("p", 2), ("p", 0), ("p", 0), ("gram", 0), ("terms", 0), ("sum", 0), ("terms", 1), ("p", 1), ("sum", 1),
+    ("sum", 0), ("p", 1), ("gram", 1), ("sum", 1), ("terms", 2), ("p", 2), ("gram", 0), ("sum", 2),
+    ("terms", 3), ("p", 2), ("gram", 2), ("sum", 3), ("terms", 4), ("sum", 4), ("sum", 2), ("terms", 5),
+    ("sum", 5), ("sum", 3), ("sum", 4), ("sum", 5), ("sum", 0), ("sum", 1), ("gram", 1), ("gram", 2),
+    ("gram", 0), ("sum", 2), ("sum", 3), ("sum", 4), ("sum", 5), ("gram", 1), ("gram", 2), ("sum", 0),
+    ("sum", 1), ("gram", 0), ("sum", 2), ("sum", 4), ("gram", 0), ("gram", 1), ("sum", 3), ("sum", 5),
+    ("gram", 2), ("gram", 1), ("gram", 2), ("factor", 2), ("sum", 0), ("sum", 1), ("factor", 2), ("sum", 2),
+    ("sum", 3), ("sum", 4), ("sum", 5), ("factor", 2), ("factor", 2), ("sum", 0), ("sum", 1), ("factor", 2),
+    ("sum", 2), ("sum", 3), ("sum", 4), ("sum", 5), ("factor", 2), ("factor", 2), ("sum", 0), ("sum", 1),
+    ("factor", 2), ("sum", 2), ("sum", 3), ("sum", 4), ("factor", 1), ("sum", 5), ("sum", 0), ("sum", 1),
+    ("factor", 1), ("sum", 2), ("sum", 3), ("sum", 4), ("factor", 1), ("sum", 5), ("sum", 0), ("sum", 1),
+    ("sum", 0), ("sum", 2), ("sum", 1), ("sum", 3), ("sum", 4), ("sum", 5), ("sum", 2), ("sum", 3),
+    ("sum", 4), ("sum", 5),
+)
 NT = (((1,), (1,)), ((), ()))
 
 
@@ -29,7 +46,7 @@
     return hi, (x - hi.astype(f32)).astype(bf16)
 
 
-def eliminate(grams, y_ref):
+def eliminate(grams, y_ref, p_ref, lhs_err, lhs_q):
     row = lax.broadcasted_iota(jnp.int32, (R, 2 * R), 0)
     lane = lax.broadcasted_iota(jnp.int32, (R, 2 * R), 1)
     eye = jnp.where(lane == row + 64, 1.0, 0.0)
@@ -79,11 +96,25 @@
         for i, (r, d) in enumerate(((r0, s00), (r1, d1), (r2, d2), (r3, d3))):
             y_ref[8 * (k + i) : 8 * (k + i) + 8] = r * (1.0 / jnp.sqrt(d))
         yield
+    wide_lane = lax.broadcasted_iota(jnp.int32, (ROWS, 2 * R), 1)
+    for m in range(MATS):
+        side = jnp.where(lane >= 64, y_ref[pl.ds(m, R, stride=8), :], 0.0)
+        other = pltpu.roll(side, 64, axis=1)
+        inverse = side if m % 2 else other
+        bh, bl = split(jnp.concatenate([inverse, inverse], axis=0))
+        ph, pl_ = split(p_ref[m // 2])
+        ortho = dot_nt(ph, bh) + (dot_nt(ph, bl) + dot_nt(pl_, bh))
+        oh, ol = split(ortho)
+        lhs_err[m] = jnp.concatenate([jnp.where(wide_lane < 64, oh, ol), oh], axis=1)
+        lh, ll = split(side + other)
+        lhs_q[m] = jnp.concatenate([jnp.where(lane < 64, lh, ll), lh], axis=1)
+        if m % 2:
+            yield
 
 
 def comm_kernel(
-    g_hbm, e_hbm, q_hbm, g_sum, p_out, y_out, ebuf,
-    gbuf, qbuf, mh, ml, qst, p_own, p_recv, p_chip, p_far, g_acc,
+    g_hbm, e_hbm, q_hbm, g_sum, lhs_err, lhs_q, ebuf,
+    p_out, y_out, gbuf, qbuf, mh, ml, qst, p_own, p_recv, p_chip, p_far, g_acc,
     core_recv, recv0, recv1, q_acc, x_acc, recv2, recv3, gram_own, gram_half, gram_recv, gram_out,
     load_sem, p_send, p_arrive, c_send, c_arrive, a_send, a_arrive, b_send, b_arrive,
     gram_send, gram_arrive,
@@ -156,31 +187,40 @@
 
     mine = pl.multiple_of(core * HALF, 8)
     theirs = pl.multiple_of((1 - core) * HALF, 8)
-    p_own[...] = jnp.zeros_like(p_own)
     qst[...] = jnp.zeros_like(qst)
     q_acc[...] = jnp.zeros_like(q_acc)
 
-    def local_p(m):
-        b = lax.rem(m, 2)
+    def arrive(m):
         for copy in loads(m):
             copy.wait()
 
-        def merge(i, _):
-            rows = pl.ds(pl.multiple_of(i * 32, 32), 32)
+    def merge(m):
+        for r in range(0, ROWS, 32):
+            rows = slice(r, r + 32)
             merged = gbuf[m, rows].astype(f32) + ebuf[m, rows]
             ebuf[m, rows] = merged
             hi, lo = split(merged)
             mh[m, rows] = hi
             ml[m, rows] = lo
-            return 0
-
-        lax.fori_loop(0, ROWS // 32, merge, 0)
+        b = m % 2
         hi, lo = split(qbuf[m])
-        at = pl.multiple_of(64 * b, 64)
-        qst[b, pl.ds(at, 64)] = hi
-        qst[b, pl.ds(at + 128, 64)] = lo
-        wide = dot_nt(mh[m], qst[b])
-        p_own[lax.div(m, 2)] += wide[:, :128] + wide[:, 128:] + dot_nt(ml[m], qst[b, :128])
+        qst[b, 64 * b : 64 * b + 64] = hi
+        qst[b, 128 + 64 * b : 192 + 64 * b] = lo
+
+    def local_p(j):
+        if j == 0:
+            arrive(0)
+            merge(0)
+        total = None
+        for m in (2 * j, 2 * j + 1):
+            if m + 1 < MATS:
+                arrive(m + 1)
+            wide = dot_nt(mh[m], qst[m % 2])
+            part = wide[:, :128] + wide[:, 128:] + dot_nt(ml[m], qst[m % 2, :128])
+            if m + 1 < MATS:
+                merge(m + 1)
+            total = part if total is None else total + part
+        p_own[j] = total
 
     def p_copy(s, j):
         if s == 0:
@@ -204,27 +244,6 @@
             p_out[j, pl.ds(mine, HALF)] = (p_chip[j] + p_far[j]) * 0.25
         if s < 3:
             p_copy(s, j).start()
-
-    def p_loop(m, _):
-        local_p(m)
-
-        @pl.when(m == 1)
-        def _():
-            pl.semaphore_wait(barrier, len(everyone))
-            p_step(0, 0)
-
-        @pl.when(m == 3)
-        def _():
-            p_step(0, 1)
-            p_step(1, 0)
-
-        @pl.when(m == 5)
-        def _():
-            p_step(0, 2)
-            p_step(1, 1)
-            p_step(2, 0)
-
-        return 0
 
     halves = {}
 
@@ -270,7 +289,7 @@
             g_acc[m, :, cols] = wide[:64] + wide[64:] + dot(top, ml[m, :, cols])
 
     def g_chain(m):
-        link = [(m + s) % 6 for s in range(6)]
+        link = [(FIRST_LINK[m] + s) % 6 for s in range(6)]
         keep = pl.multiple_of(core * 32, 32)
         give = pl.multiple_of((1 - core) * 32, 32)
         kept0 = pl.multiple_of(core * 32 + 16 * sides[link[0]], 16)
@@ -339,53 +358,26 @@
     ac = [g_chain(m) for m in range(MATS)]
     factor = None
 
-    def behind():
-        nonlocal factor
-        if factor is None:
-            if all([next(chain, 1) for chain in gc]):
-                factor = eliminate([gram_out[j] for j in range(3)], y_out)
-        if factor is not None:
-            next(factor, None)
-
-    lax.fori_loop(0, MATS, p_loop, 0)
-    p_step(1, 2)
-    p_step(3, 0)
-    next(gc[0])
-    local_g(0)
-    next(ac[0])
-    p_step(2, 1)
-    local_g(1)
-    next(ac[1])
-    p_step(2, 2)
-    p_step(3, 1)
-    next(gc[1])
-    next(gc[0])
-    local_g(2)
-    next(ac[2])
-    next(ac[0])
-    local_g(3)
-    next(ac[3])
-    next(ac[1])
-    p_step(3, 2)
-    next(gc[2])
-    next(gc[1])
-    next(gc[0])
-    local_g(4)
-    next(ac[4])
-    next(ac[2])
-    local_g(5)
-    next(ac[5])
-    next(ac[3])
-    next(gc[2])
-    next(gc[1])
-    next(gc[0])
-    next(ac[4])
-    next(ac[5])
-    for s in range(8):
-        for m in range(MATS):
-            next(ac[m], None)
-            if factor is not None or m in (2, 5):
-                behind()
+    p_stage = [0, 0, 0]
+    for what, i in ORDER:
+        if what == "products":
+            local_p(i)
+            if i == 0:
+                pl.semaphore_wait(barrier, len(everyone))
+        elif what == "p":
+            p_step(p_stage[i], i)
+            p_stage[i] += 1
+        elif what == "gram":
+            next(gc[i], None)
+        elif what == "terms":
+            local_g(i)
+        elif what == "sum":
+            next(ac[i], None)
+        else:
+            if factor is None:
+                factor = eliminate([gram_out[j] for j in range(3)], y_out, p_out, lhs_err, lhs_q)
+            for _ in range(i):
+                next(factor, None)
     for _ in factor:
         pass
     for s in range(3):
@@ -395,29 +387,14 @@
         copy.wait_send()
 
 
-def finish_kernel(
-    g_sum, p_ref, y_ref, m_ref, err_hbm, q_out, mbuf, new_q, wst, store_sem, q_sem,
-):
-    lane = lax.broadcasted_iota(jnp.int32, (R, 2 * R), 1)
-    wide_lane = lax.broadcasted_iota(jnp.int32, (ROWS, 2 * R), 1)
+def finish_kernel(g_sum, lhs_err, lhs_q, m_ref, err_hbm, q_out, ebuf, new_q, wst, store_sem, q_sem):
     stores = []
     for m in range(MATS):
-        b = m % 2
-        side = jnp.where(lane >= 64, y_ref[pl.ds(m, R, stride=8), :], 0.0)
-        other = pltpu.roll(side, 64, axis=1)
-        inverse = side if b else other
-        bh, bl = split(jnp.concatenate([inverse, inverse], axis=0))
-        ph, pl_ = split(p_ref[m // 2])
-        ortho = dot_nt(ph, bh) + (dot_nt(ph, bl) + dot_nt(pl_, bh))
-        oh, ol = split(ortho)
-        lhs = jnp.concatenate([jnp.where(wide_lane < 64, oh, ol), oh[:, :64]], axis=1)
-        lh, ll = split(side + other)
-        lhs_q = jnp.concatenate([jnp.where(lane < 64, lh, ll), lh[:, :64]], axis=1)
         gh, gl = split(g_sum[m, :, :D] * 0.25)
         wst[0, 0:64] = gh
         wst[0, 64:128] = gh
         wst[0, 128:192] = gl
-        fresh = dot(lhs_q, wst[0])
+        fresh = dot(lhs_q[m, :, :192], wst[0])
         new_q[m] = fresh
         store = pltpu.make_async_copy(new_q.at[m], q_out.at[m], q_sem.at[m])
         store.start()
@@ -426,12 +403,15 @@
         wst[1, 0:64] = nh
         wst[1, 64:128] = nh
         wst[1, 128:192] = nl
-        for start, size in COLS:
+        for i, (start, size) in enumerate(COLS):
             cols = slice(start, start + size)
-            mbuf[m, :, cols] = m_ref[m, :, cols] - dot(lhs, wst[1, :, cols])
-        store = pltpu.make_async_copy(mbuf.at[m], err_hbm.at[0, m], store_sem.at[m])
-        store.start()
-        stores.append(store)
+            ebuf[m, :, cols] = m_ref[m, :, cols] - dot(lhs_err[m, :, :192], wst[1, :, cols])
+            place = pl.ds(start, size)
+            store = pltpu.make_async_copy(
+                ebuf.at[m, :, place], err_hbm.at[0, m, :, place], store_sem.at[m, i]
+            )
+            store.start()
+            stores.append(store)
     for store in stores:
         store.wait()
 
@@ -440,17 +420,19 @@
     vmem = pl.BlockSpec(memory_space=pltpu.VMEM)
     far_hbm = pl.BlockSpec(memory_space=pltpu.HBM)
     sem = pltpu.SemaphoreType.DMA
-    g_sum, p_mat, y_mat, merged = pl.pallas_call(
+    g_sum, lhs_err, lhs_q, merged = pl.pallas_call(
         comm_kernel,
         out_shape=(
             jax.ShapeDtypeStruct((MATS, R, 4 * BLOCK), f32),
-            jax.ShapeDtypeStruct((MATS // 2, ROWS, 2 * R), f32),
-            jax.ShapeDtypeStruct((8 * R, 2 * R), f32),
+            jax.ShapeDtypeStruct((MATS, ROWS, 256), bf16),
+            jax.ShapeDtypeStruct((MATS, R, 256), bf16),
             jax.ShapeDtypeStruct((MATS, ROWS, D), f32),
         ),
         in_specs=[far_hbm, far_hbm, far_hbm],
         out_specs=(vmem, vmem, vmem, vmem),
         scratch_shapes=[
+            pltpu.VMEM((MATS // 2, ROWS, 2 * R), f32),
+            pltpu.VMEM((8 * R, 2 * R), f32),
             pltpu.VMEM((MATS, ROWS, D), bf16),
             pltpu.VMEM((MATS, R, D), f32),
             pltpu.VMEM((MATS, ROWS, D), bf16),
@@ -501,12 +483,12 @@
             pltpu.VMEM((MATS, ROWS, D), f32),
             pltpu.VMEM((MATS, R, D), f32),
             pltpu.VMEM((2, ROWS, D), bf16),
-            sem((MATS,)),
+            sem((MATS, 3)),
             sem((MATS,)),
         ],
         compiler_params=pltpu.CompilerParams(vmem_limit_bytes=24 * 2**20),
         name="new_q_and_errors",
-    )(g_sum, p_mat, y_mat, merged)
+    )(g_sum, lhs_err, lhs_q, merged)
 
 
 def solution(mesh):

time: 63.1 us -> 59.9 us (0.949)
  Pallas kernels: 62.3 us -> 59.1 us
    pallas_call x1, Pallas kernels: 58.3 us -> 55.2 us  [body(): pl.pallas_call(comm_kernel, out_shape=(jax.ShapeDtypeStruct((MATS, R, 4 *...]
where the time goes in v8:
time: 59.9 us; the launch traced here: 59.8 us
  Pallas kernels  59.1 us (99%)
  between operations  0.64 us (1%)
    pallas_call x1, Pallas kernels, body(): pl.pallas_call(comm_kernel, out_shape=(jax.ShapeDtypeStruct((MATS, R, 4 *...  55.2 us
    pallas_call x1, Pallas kernels, body(): pl.pallas_call(finish_kernel, out_shape=(jax.ShapeDtypeStruct((1, MATS, R...  3.92 us

profile of v8, /device:TPU:1, one launch (start us, length us, event | category | flops | bytes accessed | tf_op | source)
XLA Modules:
  0.0 59.8 jit_solution(10410918614744025848)
XLA Ops:
  0.6 55.2 %compress_and_sum.1 = (f32[6,64,1536]{2,1,0:T(8,128)S(1)}, bf16[6,192,256]{2,1,0:T(8,128)(2,1)S(1)}, bf16[6,64,256]{2,1,0:T(8,128)(2,1)S(1)}, f32[6,192,1408]{2,1,0:T(8,128)S(1)}) custom-call(bf16[1,6,192,1408]{3,2,1,0:T(8,128)(2,1)} %g_hbm.1, f32[1,6,192,1408]{3,2,1,0:T(8,128)} %e_hbm.1, f32[6,64,1408]{2,1,0:T(8,128)} %q_hbm.1), custom_call_target="tpu_custom_call" | custom-call | tf_op jit(solution)/shard_map/compress_and_sum/pallas_call | solution.py:423
  55.8 3.9 %new_q_and_errors.1 = (f32[1,6,192,1408]{3,2,1,0:T(8,128)}, f32[6,64,1408]{2,1,0:T(8,128)}) custom-call(f32[6,64,1536]{2,1,0:T(8,128)S(1)} %get-tuple-element.6.g_sum, bf16[6,192,256]{2,1,0:T(8,128)(2,1)S(1)} %get-tuple-element.7.lhs_err, bf16[6,64,256]{2,1,0:T(8,128)(2,1)S(1)} %get-tuple-element.8.lhs_q, f32[6,192,1408]{2,1,0:T(8,128)S(1)} %get-tuple-element.9.m_ref), custom_call_target="tpu_custom_call" | custom-call | tf_op jit(solution)/shard_map/new_q_and_errors/pallas_call | solution.py:474

commit v9 on v8

--- a/solution.py
+++ b/solution.py
@@ -13,22 +13,31 @@
 BLOCK = 384
 COLS = ((0, 512), (512, 512), (1024, 384))
 f32, bf16 = jnp.float32, jnp.bfloat16
-FIRST_LINK = (0, 3, 2, 5, 1, 4)
+LINKS = (
+    (0, 1, 3, 2, 4, 5),
+    (1, 2, 4, 0, 5, 3),
+    (2, 0, 1, 5, 3, 4),
+    (0, 1, 4, 3, 2, 5),
+    (1, 2, 0, 4, 5, 3),
+    (2, 0, 1, 5, 4, 3),
+)
+PAIRS = tuple(sorted({tuple(sorted(links[i : i + 2])) for links in LINKS for i in (2, 4)}))
 ORDER = (
     ("products", 0), ("p", 0), ("products", 1), ("p", 1), ("p", 0), ("products", 2), ("p", 2), ("p", 1),
-    ("p", 2), ("p", 0), ("p", 0), ("gram", 0), ("terms", 0), ("sum", 0), ("terms", 1), ("p", 1), ("sum", 1),
-    ("sum", 0), ("p", 1), ("gram", 1), ("sum", 1), ("terms", 2), ("p", 2), ("gram", 0), ("sum", 2),
-    ("terms", 3), ("p", 2), ("gram", 2), ("sum", 3), ("terms", 4), ("sum", 4), ("sum", 2), ("terms", 5),
-    ("sum", 5), ("sum", 3), ("sum", 4), ("sum", 5), ("sum", 0), ("sum", 1), ("gram", 1), ("gram", 2),
-    ("gram", 0), ("sum", 2), ("sum", 3), ("sum", 4), ("sum", 5), ("gram", 1), ("gram", 2), ("sum", 0),
-    ("sum", 1), ("gram", 0), ("sum", 2), ("sum", 4), ("gram", 0), ("gram", 1), ("sum", 3), ("sum", 5),
-    ("gram", 2), ("gram", 1), ("gram", 2), ("factor", 2), ("sum", 0), ("sum", 1), ("factor", 2), ("sum", 2),
-    ("sum", 3), ("sum", 4), ("sum", 5), ("factor", 2), ("factor", 2), ("sum", 0), ("sum", 1), ("factor", 2),
-    ("sum", 2), ("sum", 3), ("sum", 4), ("sum", 5), ("factor", 2), ("factor", 2), ("sum", 0), ("sum", 1),
-    ("factor", 2), ("sum", 2), ("sum", 3), ("sum", 4), ("factor", 1), ("sum", 5), ("sum", 0), ("sum", 1),
-    ("factor", 1), ("sum", 2), ("sum", 3), ("sum", 4), ("factor", 1), ("sum", 5), ("sum", 0), ("sum", 1),
-    ("sum", 0), ("sum", 2), ("sum", 1), ("sum", 3), ("sum", 4), ("sum", 5), ("sum", 2), ("sum", 3),
-    ("sum", 4), ("sum", 5),
+    ("p", 2), ("p", 0), ("p", 0), ("terms", 0), ("sum", 0), ("terms", 1), ("p", 1), ("sum", 1), ("gram", 0),
+    ("sum", 0), ("p", 1), ("terms", 2), ("sum", 2), ("sum", 1), ("terms", 3), ("p", 2), ("sum", 3),
+    ("gram", 1), ("sum", 2), ("gram", 0), ("p", 2), ("terms", 4), ("sum", 4), ("sum", 3), ("sum", 0),
+    ("terms", 5), ("sum", 5), ("gram", 2), ("sum", 4), ("sum", 1), ("gram", 1), ("sum", 5), ("sum", 2),
+    ("gram", 0), ("sum", 0), ("gram", 2), ("sum", 3), ("sum", 1), ("gram", 1), ("sum", 2), ("sum", 4),
+    ("gram", 0), ("gram", 2), ("sum", 5), ("sum", 3), ("sum", 0), ("gram", 1), ("sum", 1), ("sum", 2),
+    ("sum", 4), ("sum", 5), ("gram", 2), ("gram", 0), ("gram", 1), ("sum", 3), ("sum", 0), ("sum", 4),
+    ("sum", 1), ("gram", 1), ("gram", 0), ("sum", 2), ("sum", 5), ("gram", 1), ("gram", 2), ("gram", 0),
+    ("sum", 3), ("sum", 0), ("sum", 1), ("sum", 4), ("sum", 2), ("sum", 5), ("gram", 2), ("sum", 0),
+    ("sum", 3), ("gram", 2), ("factor", 2), ("sum", 4), ("sum", 1), ("sum", 2), ("factor", 2), ("sum", 5),
+    ("factor", 2), ("sum", 3), ("factor", 2), ("sum", 4), ("sum", 0), ("factor", 2), ("sum", 5), ("sum", 1),
+    ("sum", 0), ("factor", 2), ("sum", 2), ("sum", 1), ("factor", 2), ("sum", 2), ("factor", 2),
+    ("factor", 1), ("factor", 1), ("factor", 1), ("sum", 3), ("sum", 4), ("sum", 5), ("sum", 3), ("sum", 4),
+    ("sum", 5),
 )
 NT = (((1,), (1,)), ((), ()))
 
@@ -131,30 +140,26 @@
     def flip(v):
         return v + 1 - 2 * lax.rem(v, 2)
 
-    def side0(v):
-        hi = lax.div(v, 2)
-        lo = lax.rem(v, 2)
-        return hi + lo - 2 * hi * lo
-
-    def side1(v):
-        return lax.div(v, 2)
+    sides = (lax.rem(x, 2), lax.rem(y, 2), lax.rem(z, 2), lax.div(x, 2), lax.div(y, 2), lax.div(z, 2))
+
+    def across(v):
+        return lax.rem(v + 2, 4)
 
     def over(*links):
         xx, yy, zz = x, y, z
         for link in links:
             if link % 3 == 0:
-                xx = flip(x) if link == 0 else 3 - x
+                xx = flip(xx) if link == 0 else across(xx)
             elif link % 3 == 1:
-                yy = flip(y) if link == 1 else 3 - y
+                yy = flip(yy) if link == 1 else across(yy)
             else:
-                zz = flip(z) if link == 2 else 3 - z
+                zz = flip(zz) if link == 2 else across(zz)
         return device(xx, yy, zz, core)
 
     near = tuple(over(link) for link in range(6))
-    corner = tuple(over(link, (link + 1) % 6) for link in range(6))
-    sides = (side0(x), side0(y), side0(z), side1(x), side1(y), side1(z))
+    corner = {pair: over(*pair) for pair in PAIRS}
     twin = device(x, y, z, 1 - core)
-    far = device(x, lax.rem(y + 2, 4), z, core)
+    far = near[4]
 
     def loads(m):
         return (
@@ -170,7 +175,7 @@
 
     lax.fori_loop(0, MATS, begin, 0)
     barrier = pltpu.get_barrier_semaphore()
-    everyone = near + corner + (twin, far)
+    everyone = near + tuple(corner.values()) + (twin,)
     for other in everyone:
         pl.semaphore_signal(barrier, inc=1, device_id=other, device_id_type=MESH)
 
@@ -247,40 +252,42 @@
 
     halves = {}
 
-    def three(src, dst, send, arrive, link):
-        targets = (near[(link + 1) % 6], near[link], corner[link])
-        return [remote(src(f), dst.at[f], send.at[f], arrive.at[f], targets[f]) for f in range(3)]
+    def transposed(j):
+        if j not in halves:
+            halves[j] = split(p_out[j].T)
+        return halves[j]
+
+    def three(src, dst, send, arrive, a, b):
+        targets = (near[b], near[a], corner[min(a, b), max(a, b)])
+        return [remote(src(f), dst(f), send.at[f], arrive.at[f], targets[f]) for f in range(3)]
 
     def gram_chain(j):
-        halves[j] = hi, lo = split(p_out[j].T)
+        hi, lo = transposed(j)
         square = dot_nt(hi, hi) + (dot_nt(hi, lo) + dot_nt(lo, hi))
         lane = lax.broadcasted_iota(jnp.int32, (R, 2 * R), 1)
         gram_own[j] = jnp.where(lane < 64, square[:64], square[64:])
         rows = pl.ds(pl.multiple_of(core * 32, 32), 32)
         gram_half[j, 0] = gram_own[j, rows]
-        for s, link in enumerate((2, 5) if j % 2 == 0 else (5, 2)):
-            copies = three(
-                lambda f: gram_half.at[j, s], gram_recv.at[j, s], gram_send.at[j, s], gram_arrive.at[j, s], link,
+        order = (0, 2, 3, 5, 1)
+        for s in range(5):
+            copy = remote(
+                gram_half.at[j, s], gram_recv.at[j, s], gram_send.at[j, s], gram_arrive.at[j, s],
+                near[order[(s + 2 * j) % 5]],
             )
             yield
-            for copy in copies:
-                copy.wait_recv()
-            got = gram_recv.at[j, s]
-            gram_half[j, s + 1] = (gram_half[j, s] + got[1]) + (got[0] + got[2])
-        copy = remote(
-            gram_half.at[j, 2], gram_recv.at[j, 2, 0], gram_send.at[j, 2, 0], gram_arrive.at[j, 2, 0], near[1],
-        )
-        yield
-        copy.wait_recv()
-        gram_out[j, rows] = gram_half[j, 2] + gram_recv[j, 2, 0]
+            copy.wait_recv()
+            total = gram_half[j, s] + gram_recv[j, s]
+            if s < 4:
+                gram_half[j, s + 1] = total
+        gram_out[j, rows] = total
         part = gram_out.at[j, rows]
-        copy = remote(part, part, gram_send.at[j, 2, 1], gram_arrive.at[j, 2, 1], twin)
+        copy = remote(part, part, gram_send.at[j, 5], gram_arrive.at[j, 5], twin)
         yield
         copy.wait_recv()
 
     def local_g(m):
         j, b = divmod(m, 2)
-        hi, lo = halves[j]
+        hi, lo = transposed(j)
         top = hi[64 * b : 64 * b + 64]
         both = jnp.concatenate([top, lo[64 * b : 64 * b + 64]], axis=0)
         for start, size in COLS:
@@ -289,7 +296,7 @@
             g_acc[m, :, cols] = wide[:64] + wide[64:] + dot(top, ml[m, :, cols])
 
     def g_chain(m):
-        link = [(FIRST_LINK[m] + s) % 6 for s in range(6)]
+        link = LINKS[m]
         keep = pl.multiple_of(core * 32, 32)
         give = pl.multiple_of((1 - core) * 32, 32)
         kept0 = pl.multiple_of(core * 32 + 16 * sides[link[0]], 16)
@@ -323,19 +330,23 @@
         yield
         copy.wait_recv()
         q_acc[m, :, :D] = g_acc[m, pl.ds(kept1, 8)] + recv1[m]
-        copies = three(lambda f: q_acc.at[m, :, others[f]], recv2.at[m], b_send.at[0, m], b_arrive.at[0, m], link[2])
+        copies = three(
+            lambda f: q_acc.at[m, :, others[f]], lambda f: recv2.at[m, f], b_send.at[0, m], b_arrive.at[0, m],
+            link[2], link[3],
+        )
         yield
         for copy in copies:
             copy.wait_recv()
         x_acc[m] = (q_acc[m, :, own] + recv2[m, 1]) + (recv2[m, 0] + recv2[m, 2])
-        copies = three(lambda f: x_acc.at[m], recv3.at[m], b_send.at[1, m], b_arrive.at[1, m], link[4])
+        copies = three(
+            lambda f: x_acc.at[m], lambda f: recv3.at[m, f], b_send.at[1, m], b_arrive.at[1, m], link[4], link[5],
+        )
         yield
         for copy in copies:
             copy.wait_recv()
         g_sum[m, pl.ds(kept1, 8), own] = (x_acc[m] + recv3[m, 1]) + (recv3[m, 0] + recv3[m, 2])
         part = g_sum.at[m, pl.ds(kept1, 8), own]
-        targets = (near[link[3]], near[link[2]], corner[link[2]])
-        copies = [remote(part, part, b_send.at[2, m, f], b_arrive.at[2, m, f], targets[f]) for f in range(3)]
+        copies = three(lambda f: part, lambda f: part, b_send.at[2, m], b_arrive.at[2, m], link[2], link[3])
         yield
         for copy in copies:
             copy.wait_recv()
@@ -451,8 +462,8 @@
             pltpu.VMEM((MATS, 3, 8, BLOCK), f32),
             pltpu.VMEM((MATS, 3, 8, BLOCK), f32),
             pltpu.VMEM((MATS // 2, R, 2 * R), f32),
-            pltpu.VMEM((MATS // 2, 3, R // 2, 2 * R), f32),
-            pltpu.VMEM((MATS // 2, 3, 3, R // 2, 2 * R), f32),
+            pltpu.VMEM((MATS // 2, 5, R // 2, 2 * R), f32),
+            pltpu.VMEM((MATS // 2, 5, R // 2, 2 * R), f32),
             pltpu.VMEM((MATS // 2, R, 2 * R), f32),
             sem((MATS, 3)),
             sem((3, 3)),
@@ -463,8 +474,8 @@
             sem((4, MATS)),
             sem((3, MATS, 3)),
             sem((3, MATS, 3)),
-            sem((3, 3, 3)),
-            sem((3, 3, 3)),
+            sem((3, 6)),
+            sem((3, 6)),
         ],
         compiler_params=pltpu.CompilerParams(
             collective_id=0, has_side_effects=True, vmem_limit_bytes=40 * 2**20

time: 59.9 us -> 60.4 us (level)
  no operation moved by 1% of the time
where the time goes in v9:
time: 60.4 us; the launch traced here: 60.3 us
  Pallas kernels  59.7 us (99%)
  between operations  0.64 us (1%)
    pallas_call x1, Pallas kernels, body(): pl.pallas_call(comm_kernel, out_shape=(jax.ShapeDtypeStruct((MATS, R, 4 *...  55.8 us
    pallas_call x1, Pallas kernels, body(): pl.pallas_call(finish_kernel, out_shape=(jax.ShapeDtypeStruct((1, MATS, R...  3.92 us

profile of v9, /device:TPU:1, one launch (start us, length us, event | category | flops | bytes accessed | tf_op | source)
XLA Modules:
  0.0 60.3 jit_solution(940222373642968270)
XLA Ops:
  0.6 55.8 %compress_and_sum.1 = (f32[6,64,1536]{2,1,0:T(8,128)S(1)}, bf16[6,192,256]{2,1,0:T(8,128)(2,1)S(1)}, bf16[6,64,256]{2,1,0:T(8,128)(2,1)S(1)}, f32[6,192,1408]{2,1,0:T(8,128)S(1)}) custom-call(bf16[1,6,192,1408]{3,2,1,0:T(8,128)(2,1)} %g_hbm.1, f32[1,6,192,1408]{3,2,1,0:T(8,128)} %e_hbm.1, f32[6,64,1408]{2,1,0:T(8,128)} %q_hbm.1), custom_call_target="tpu_custom_call" | custom-call | tf_op jit(solution)/shard_map/compress_and_sum/pallas_call | solution.py:434
  56.4 3.9 %new_q_and_errors.1 = (f32[1,6,192,1408]{3,2,1,0:T(8,128)}, f32[6,64,1408]{2,1,0:T(8,128)}) custom-call(f32[6,64,1536]{2,1,0:T(8,128)S(1)} %get-tuple-element.6.g_sum, bf16[6,192,256]{2,1,0:T(8,128)(2,1)S(1)} %get-tuple-element.7.lhs_err, bf16[6,64,256]{2,1,0:T(8,128)(2,1)S(1)} %get-tuple-element.8.lhs_q, f32[6,192,1408]{2,1,0:T(8,128)S(1)} %get-tuple-element.9.m_ref), custom_call_target="tpu_custom_call" | custom-call | tf_op jit(solution)/shard_map/new_q_and_errors/pallas_call | solution.py:485

commit v10 on v8

--- a/solution.py
+++ b/solution.py
@@ -13,22 +13,31 @@
 BLOCK = 384
 COLS = ((0, 512), (512, 512), (1024, 384))
 f32, bf16 = jnp.float32, jnp.bfloat16
-FIRST_LINK = (0, 3, 2, 5, 1, 4)
+LINKS = (
+    (1, 2, 4, 3, 5, 0),
+    (3, 4, 1, 2, 5, 0),
+    (0, 5, 1, 2, 4, 3),
+    (0, 5, 3, 4, 2, 1),
+    (4, 3, 2, 1, 0, 5),
+    (2, 1, 5, 0, 3, 4),
+)
+GRAM_PAIRS = ((2, 3), (5, 0))
+PAIRS = tuple(sorted({tuple(sorted(links[i : i + 2])) for links in LINKS + GRAM_PAIRS for i in range(0, len(links), 2)}))
 ORDER = (
     ("products", 0), ("p", 0), ("products", 1), ("p", 1), ("p", 0), ("products", 2), ("p", 2), ("p", 1),
-    ("p", 2), ("p", 0), ("p", 0), ("gram", 0), ("terms", 0), ("sum", 0), ("terms", 1), ("p", 1), ("sum", 1),
-    ("sum", 0), ("p", 1), ("gram", 1), ("sum", 1), ("terms", 2), ("p", 2), ("gram", 0), ("sum", 2),
-    ("terms", 3), ("p", 2), ("gram", 2), ("sum", 3), ("terms", 4), ("sum", 4), ("sum", 2), ("terms", 5),
-    ("sum", 5), ("sum", 3), ("sum", 4), ("sum", 5), ("sum", 0), ("sum", 1), ("gram", 1), ("gram", 2),
-    ("gram", 0), ("sum", 2), ("sum", 3), ("sum", 4), ("sum", 5), ("gram", 1), ("gram", 2), ("sum", 0),
-    ("sum", 1), ("gram", 0), ("sum", 2), ("sum", 4), ("gram", 0), ("gram", 1), ("sum", 3), ("sum", 5),
-    ("gram", 2), ("gram", 1), ("gram", 2), ("factor", 2), ("sum", 0), ("sum", 1), ("factor", 2), ("sum", 2),
-    ("sum", 3), ("sum", 4), ("sum", 5), ("factor", 2), ("factor", 2), ("sum", 0), ("sum", 1), ("factor", 2),
-    ("sum", 2), ("sum", 3), ("sum", 4), ("sum", 5), ("factor", 2), ("factor", 2), ("sum", 0), ("sum", 1),
-    ("factor", 2), ("sum", 2), ("sum", 3), ("sum", 4), ("factor", 1), ("sum", 5), ("sum", 0), ("sum", 1),
-    ("factor", 1), ("sum", 2), ("sum", 3), ("sum", 4), ("factor", 1), ("sum", 5), ("sum", 0), ("sum", 1),
-    ("sum", 0), ("sum", 2), ("sum", 1), ("sum", 3), ("sum", 4), ("sum", 5), ("sum", 2), ("sum", 3),
-    ("sum", 4), ("sum", 5),
+    ("p", 2), ("p", 0), ("p", 0), ("terms", 0), ("p", 1), ("sum", 0), ("terms", 1), ("sum", 1), ("gram", 0),
+    ("p", 1), ("terms", 2), ("p", 2), ("sum", 2), ("sum", 0), ("sum", 1), ("terms", 3), ("sum", 3),
+    ("gram", 1), ("p", 2), ("terms", 4), ("sum", 4), ("sum", 2), ("terms", 5), ("sum", 5), ("sum", 3),
+    ("gram", 2), ("gram", 0), ("sum", 4), ("sum", 5), ("sum", 0), ("gram", 1), ("sum", 1), ("gram", 2),
+    ("sum", 2), ("sum", 5), ("sum", 4), ("sum", 3), ("sum", 0), ("sum", 1), ("gram", 0), ("gram", 1),
+    ("sum", 2), ("gram", 2), ("sum", 4), ("sum", 5), ("gram", 0), ("sum", 3), ("gram", 1), ("sum", 0),
+    ("gram", 2), ("sum", 1), ("gram", 0), ("sum", 2), ("gram", 1), ("gram", 2), ("factor", 1), ("factor", 1),
+    ("sum", 4), ("sum", 3), ("sum", 5), ("factor", 1), ("sum", 0), ("sum", 1), ("sum", 2), ("factor", 1),
+    ("factor", 1), ("factor", 1), ("sum", 4), ("factor", 1), ("sum", 3), ("sum", 5), ("factor", 1),
+    ("factor", 1), ("sum", 0), ("factor", 1), ("factor", 1), ("sum", 1), ("sum", 2), ("sum", 0),
+    ("factor", 1), ("factor", 1), ("sum", 1), ("factor", 1), ("sum", 4), ("sum", 5), ("sum", 2),
+    ("factor", 1), ("sum", 3), ("factor", 1), ("factor", 1), ("factor", 1), ("factor", 1), ("sum", 4),
+    ("sum", 5), ("sum", 3),
 )
 NT = (((1,), (1,)), ((), ()))
 
@@ -115,8 +124,8 @@
 def comm_kernel(
     g_hbm, e_hbm, q_hbm, g_sum, lhs_err, lhs_q, ebuf,
     p_out, y_out, gbuf, qbuf, mh, ml, qst, p_own, p_recv, p_chip, p_far, g_acc,
-    core_recv, recv0, recv1, q_acc, x_acc, recv2, recv3, gram_own, gram_half, gram_recv, gram_out,
-    load_sem, p_send, p_arrive, c_send, c_arrive, a_send, a_arrive, b_send, b_arrive,
+    core_recv, recv1, q_acc, x_acc, recv2, recv3, gram_own, gram_half, gram_recv, gram_out,
+    load_sem, p_send, p_arrive, c_send, c_arrive, a_send, a_arrive,
     gram_send, gram_arrive,
 ):
     dp, mp = lax.axis_index("dp"), lax.axis_index("mp")
@@ -151,7 +160,7 @@
         return device(xx, yy, zz, core)
 
     near = tuple(over(link) for link in range(6))
-    corner = tuple(over(link, (link + 1) % 6) for link in range(6))
+    corner = {pair: over(*pair) for pair in PAIRS}
     sides = (side0(x), side0(y), side0(z), side1(x), side1(y), side1(z))
     twin = device(x, y, z, 1 - core)
     far = device(x, lax.rem(y + 2, 4), z, core)
@@ -170,7 +179,7 @@
 
     lax.fori_loop(0, MATS, begin, 0)
     barrier = pltpu.get_barrier_semaphore()
-    everyone = near + corner + (twin, far)
+    everyone = near + tuple(corner.values()) + (twin, far)
     for other in everyone:
         pl.semaphore_signal(barrier, inc=1, device_id=other, device_id_type=MESH)
 
@@ -247,20 +256,26 @@
 
     halves = {}
 
-    def three(src, dst, send, arrive, link):
-        targets = (near[(link + 1) % 6], near[link], corner[link])
-        return [remote(src(f), dst.at[f], send.at[f], arrive.at[f], targets[f]) for f in range(3)]
+    def transposed(j):
+        if j not in halves:
+            halves[j] = split(p_out[j].T)
+        return halves[j]
+
+    def three(src, dst, send, arrive, a, b):
+        targets = (near[b], near[a], corner[min(a, b), max(a, b)])
+        return [remote(src(f), dst(f), send.at[f], arrive.at[f], targets[f]) for f in range(3)]
 
     def gram_chain(j):
-        halves[j] = hi, lo = split(p_out[j].T)
+        hi, lo = transposed(j)
         square = dot_nt(hi, hi) + (dot_nt(hi, lo) + dot_nt(lo, hi))
         lane = lax.broadcasted_iota(jnp.int32, (R, 2 * R), 1)
         gram_own[j] = jnp.where(lane < 64, square[:64], square[64:])
         rows = pl.ds(pl.multiple_of(core * 32, 32), 32)
         gram_half[j, 0] = gram_own[j, rows]
-        for s, link in enumerate((2, 5) if j % 2 == 0 else (5, 2)):
+        for s, (one, two) in enumerate(GRAM_PAIRS if j % 2 == 0 else GRAM_PAIRS[::-1]):
             copies = three(
-                lambda f: gram_half.at[j, s], gram_recv.at[j, s], gram_send.at[j, s], gram_arrive.at[j, s], link,
+                lambda f: gram_half.at[j, s], lambda f: gram_recv.at[j, s, f], gram_send.at[j, s], gram_arrive.at[j, s],
+                one, two,
             )
             yield
             for copy in copies:
@@ -280,7 +295,7 @@
 
     def local_g(m):
         j, b = divmod(m, 2)
-        hi, lo = halves[j]
+        hi, lo = transposed(j)
         top = hi[64 * b : 64 * b + 64]
         both = jnp.concatenate([top, lo[64 * b : 64 * b + 64]], axis=0)
         for start, size in COLS:
@@ -289,70 +304,63 @@
             g_acc[m, :, cols] = wide[:64] + wide[64:] + dot(top, ml[m, :, cols])
 
     def g_chain(m):
-        link = [(FIRST_LINK[m] + s) % 6 for s in range(6)]
+        link = LINKS[m]
         keep = pl.multiple_of(core * 32, 32)
         give = pl.multiple_of((1 - core) * 32, 32)
-        kept0 = pl.multiple_of(core * 32 + 16 * sides[link[0]], 16)
-        gone0 = pl.multiple_of(core * 32 + 16 - 16 * sides[link[0]], 16)
-        kept1 = pl.multiple_of(kept0 + 8 * sides[link[1]], 8)
-        gone1 = pl.multiple_of(kept0 + 8 - 8 * sides[link[1]], 8)
-        hi, lo = sides[link[2]], sides[link[3]]
+
+        def both_ways(place, i):
+            hi, lo = sides[link[i]], sides[link[i + 1]]
+            return place(hi, lo), (place(hi, 1 - lo), place(1 - hi, lo), place(1 - hi, 1 - lo))
+
+        def tile(h, l):
+            return pl.ds(pl.multiple_of(core * 32 + (2 * h + l) * 8, 8), 8)
 
         def block(h, l):
             return pl.ds(pl.multiple_of((2 * h + l) * BLOCK, 128), BLOCK)
 
-        own = block(hi, lo)
-        others = (block(hi, 1 - lo), block(1 - hi, lo), block(1 - hi, 1 - lo))
+        rows, other_rows = both_ways(tile, 0)
+        own, others = both_ways(block, 2)
+        far_rows = pl.ds(pl.multiple_of(core * 32 + 16 - 16 * sides[link[0]], 16), 16)
 
         def send(s, src, dst, i):
-            return remote(src, dst, a_send.at[s, m], a_arrive.at[s, m], near[link[i]])
-
-        def forward(i, row, size):
-            part = g_sum.at[m, pl.ds(row, size), pl.ds(0, D)]
+            return three(src, dst, a_send.at[s, m], a_arrive.at[s, m], link[i], link[i + 1])
+
+        def forward(i, where):
+            part = g_sum.at[m, where, pl.ds(0, D)]
             return remote(part, part, c_send.at[i, m], c_arrive.at[i, m], twin)
+
+        def wait(copies):
+            for copy in copies:
+                copy.wait_recv()
 
         copy = remote(g_acc.at[m, pl.ds(give, 32)], core_recv.at[m], c_send.at[0, m], c_arrive.at[0, m], twin)
         yield
         copy.wait_recv()
         g_acc[m, pl.ds(keep, 32)] += core_recv[m]
-        copy = send(0, g_acc.at[m, pl.ds(gone0, 16)], recv0.at[m], 0)
-        yield
-        copy.wait_recv()
-        g_acc[m, pl.ds(kept0, 16)] += recv0[m]
-        copy = send(1, g_acc.at[m, pl.ds(gone1, 8)], recv1.at[m], 1)
-        yield
-        copy.wait_recv()
-        q_acc[m, :, :D] = g_acc[m, pl.ds(kept1, 8)] + recv1[m]
-        copies = three(lambda f: q_acc.at[m, :, others[f]], recv2.at[m], b_send.at[0, m], b_arrive.at[0, m], link[2])
-        yield
-        for copy in copies:
-            copy.wait_recv()
+        copies = send(0, lambda f: g_acc.at[m, other_rows[f]], lambda f: recv1.at[m, f], 0)
+        yield
+        wait(copies)
+        q_acc[m, :, :D] = (g_acc[m, rows] + recv1[m, 1]) + (recv1[m, 0] + recv1[m, 2])
+        copies = send(1, lambda f: q_acc.at[m, :, others[f]], lambda f: recv2.at[m, f], 2)
+        yield
+        wait(copies)
         x_acc[m] = (q_acc[m, :, own] + recv2[m, 1]) + (recv2[m, 0] + recv2[m, 2])
-        copies = three(lambda f: x_acc.at[m], recv3.at[m], b_send.at[1, m], b_arrive.at[1, m], link[4])
-        yield
-        for copy in copies:
-            copy.wait_recv()
-        g_sum[m, pl.ds(kept1, 8), own] = (x_acc[m] + recv3[m, 1]) + (recv3[m, 0] + recv3[m, 2])
-        part = g_sum.at[m, pl.ds(kept1, 8), own]
-        targets = (near[link[3]], near[link[2]], corner[link[2]])
-        copies = [remote(part, part, b_send.at[2, m, f], b_arrive.at[2, m, f], targets[f]) for f in range(3)]
-        yield
-        for copy in copies:
-            copy.wait_recv()
-        part = g_sum.at[m, pl.ds(kept1, 8), pl.ds(0, D)]
-        copy = send(2, part, part, 1)
-        passed = [forward(1, kept1, 8)]
-        yield
-        copy.wait_recv()
-        part = g_sum.at[m, pl.ds(kept0, 16), pl.ds(0, D)]
-        copy = send(3, part, part, 0)
-        passed.append(forward(2, gone1, 8))
-        yield
-        copy.wait_recv()
-        passed.append(forward(3, gone0, 16))
-        yield
-        for copy in passed:
-            copy.wait_recv()
+        copies = send(2, lambda f: x_acc.at[m], lambda f: recv3.at[m, f], 4)
+        yield
+        wait(copies)
+        g_sum[m, rows, own] = (x_acc[m] + recv3[m, 1]) + (recv3[m, 0] + recv3[m, 2])
+        part = g_sum.at[m, rows, own]
+        copies = send(3, lambda f: part, lambda f: part, 2)
+        yield
+        wait(copies)
+        whole = g_sum.at[m, rows, pl.ds(0, D)]
+        copies = send(4, lambda f: whole, lambda f: whole, 0)
+        passed = [forward(1, rows)]
+        yield
+        wait(copies)
+        passed += [forward(2, other_rows[0]), forward(3, far_rows)]
+        yield
+        wait(passed)
 
     gc = [gram_chain(j) for j in range(3)]
     ac = [g_chain(m) for m in range(MATS)]
@@ -444,8 +452,7 @@
             pltpu.VMEM((MATS // 2, HALF, 128), f32),
             pltpu.VMEM((MATS, R, D), f32),
             pltpu.VMEM((MATS, 32, D), f32),
-            pltpu.VMEM((MATS, 16, D), f32),
-            pltpu.VMEM((MATS, 8, D), f32),
+            pltpu.VMEM((MATS, 3, 8, D), f32),
             pltpu.VMEM((MATS, 8, 4 * BLOCK), f32),
             pltpu.VMEM((MATS, 8, BLOCK), f32),
             pltpu.VMEM((MATS, 3, 8, BLOCK), f32),
@@ -459,10 +466,8 @@
             sem((3, 3)),
             sem((4, MATS)),
             sem((4, MATS)),
-            sem((4, MATS)),
-            sem((4, MATS)),
-            sem((3, MATS, 3)),
-            sem((3, MATS, 3)),
+            sem((5, MATS, 3)),
+            sem((5, MATS, 3)),
             sem((3, 3, 3)),
             sem((3, 3, 3)),
         ],

time: 59.9 us -> 51.3 us (0.86)
  Pallas kernels: 59.1 us -> 50.6 us
    pallas_call x1, Pallas kernels: 55.2 us -> 46.6 us  [body(): pl.pallas_call(comm_kernel, out_shape=(jax.ShapeDtypeStruct((MATS, R, 4 *...]
where the time goes in v10:
time: 51.3 us; the launch traced here: 51.2 us
  Pallas kernels  50.6 us (99%)
  between operations  0.64 us (1%)
    pallas_call x1, Pallas kernels, body(): pl.pallas_call(comm_kernel, out_shape=(jax.ShapeDtypeStruct((MATS, R, 4 *...  46.6 us
    pallas_call x1, Pallas kernels, body(): pl.pallas_call(finish_kernel, out_shape=(jax.ShapeDtypeStruct((1, MATS, R...  3.92 us

profile of v10, /device:TPU:1, one launch (start us, length us, event | category | flops | bytes accessed | tf_op | source)
XLA Modules:
  0.0 51.2 jit_solution(16340884903783488618)
XLA Ops:
  0.6 46.6 %compress_and_sum.1 = (f32[6,64,1536]{2,1,0:T(8,128)S(1)}, bf16[6,192,256]{2,1,0:T(8,128)(2,1)S(1)}, bf16[6,64,256]{2,1,0:T(8,128)(2,1)S(1)}, f32[6,192,1408]{2,1,0:T(8,128)S(1)}) custom-call(bf16[1,6,192,1408]{3,2,1,0:T(8,128)(2,1)} %g_hbm.1, f32[1,6,192,1408]{3,2,1,0:T(8,128)} %e_hbm.1, f32[6,64,1408]{2,1,0:T(8,128)} %q_hbm.1), custom_call_target="tpu_custom_call" | custom-call | tf_op jit(solution)/shard_map/compress_and_sum/pallas_call | solution.py:431
  47.3 3.9 %new_q_and_errors.1 = (f32[1,6,192,1408]{3,2,1,0:T(8,128)}, f32[6,64,1408]{2,1,0:T(8,128)}) custom-call(f32[6,64,1536]{2,1,0:T(8,128)S(1)} %get-tuple-element.6.g_sum, bf16[6,192,256]{2,1,0:T(8,128)(2,1)S(1)} %get-tuple-element.7.lhs_err, bf16[6,64,256]{2,1,0:T(8,128)(2,1)S(1)} %get-tuple-element.8.lhs_q, f32[6,192,1408]{2,1,0:T(8,128)S(1)} %get-tuple-element.9.m_ref), custom_call_target="tpu_custom_call" | custom-call | tf_op jit(solution)/shard_map/new_q_and_errors/pallas_call | solution.py:479

commit v11 on v10

--- a/solution.py
+++ b/solution.py
@@ -11,6 +11,7 @@
 MATS, ROWS, D, R = 6, 192, 1408, 64
 HALF = ROWS // 2
 BLOCK = 384
+AHEAD = 3
 COLS = ((0, 512), (512, 512), (1024, 384))
 f32, bf16 = jnp.float32, jnp.bfloat16
 LINKS = (
@@ -177,7 +178,7 @@
             copy.start()
         return 0
 
-    lax.fori_loop(0, MATS, begin, 0)
+    lax.fori_loop(0, AHEAD, begin, 0)
     barrier = pltpu.get_barrier_semaphore()
     everyone = near + tuple(corner.values()) + (twin, far)
     for other in everyone:
@@ -219,11 +220,14 @@
     def local_p(j):
         if j == 0:
             arrive(0)
+            begin(AHEAD, 0)
             merge(0)
         total = None
         for m in (2 * j, 2 * j + 1):
             if m + 1 < MATS:
                 arrive(m + 1)
+                if m + 1 + AHEAD < MATS:
+                    begin(m + 1 + AHEAD, 0)
             wide = dot_nt(mh[m], qst[m % 2])
             part = wide[:, :128] + wide[:, 128:] + dot_nt(ml[m], qst[m % 2, :128])
             if m + 1 < MATS:

time: 51.3 us -> 51.5 us (level)
  no operation moved by 1% of the time
where the time goes in v11:
time: 51.5 us; the launch traced here: 51.4 us
  Pallas kernels  50.8 us (99%)
  between operations  0.64 us (1%)
    pallas_call x1, Pallas kernels, body(): pl.pallas_call(comm_kernel, out_shape=(jax.ShapeDtypeStruct((MATS, R, 4 *...  46.9 us
    pallas_call x1, Pallas kernels, body(): pl.pallas_call(finish_kernel, out_shape=(jax.ShapeDtypeStruct((1, MATS, R...  3.92 us

profile of v11, /device:TPU:1, one launch (start us, length us, event | category | flops | bytes accessed | tf_op | source)
XLA Modules:
  0.0 51.4 jit_solution(54450897207279856)
XLA Ops:
  0.6 46.9 %compress_and_sum.1 = (f32[6,64,1536]{2,1,0:T(8,128)S(1)}, bf16[6,192,256]{2,1,0:T(8,128)(2,1)S(1)}, bf16[6,64,256]{2,1,0:T(8,128)(2,1)S(1)}, f32[6,192,1408]{2,1,0:T(8,128)S(1)}) custom-call(bf16[1,6,192,1408]{3,2,1,0:T(8,128)(2,1)} %g_hbm.1, f32[1,6,192,1408]{3,2,1,0:T(8,128)} %e_hbm.1, f32[6,64,1408]{2,1,0:T(8,128)} %q_hbm.1), custom_call_target="tpu_custom_call" | custom-call | tf_op jit(solution)/shard_map/compress_and_sum/pallas_call | solution.py:435
  47.5 3.9 %new_q_and_errors.1 = (f32[1,6,192,1408]{3,2,1,0:T(8,128)}, f32[6,64,1408]{2,1,0:T(8,128)}) custom-call(f32[6,64,1536]{2,1,0:T(8,128)S(1)} %get-tuple-element.6.g_sum, bf16[6,192,256]{2,1,0:T(8,128)(2,1)S(1)} %get-tuple-element.7.lhs_err, bf16[6,64,256]{2,1,0:T(8,128)(2,1)S(1)} %get-tuple-element.8.lhs_q, f32[6,192,1408]{2,1,0:T(8,128)S(1)} %get-tuple-element.9.m_ref), custom_call_target="tpu_custom_call" | custom-call | tf_op jit(solution)/shard_map/new_q_and_errors/pallas_call | solution.py:483

commit v12 on v10

--- a/solution.py
+++ b/solution.py
@@ -15,29 +15,29 @@
 f32, bf16 = jnp.float32, jnp.bfloat16
 LINKS = (
     (1, 2, 4, 3, 5, 0),
-    (3, 4, 1, 2, 5, 0),
-    (0, 5, 1, 2, 4, 3),
-    (0, 5, 3, 4, 2, 1),
-    (4, 3, 2, 1, 0, 5),
-    (2, 1, 5, 0, 3, 4),
+    (5, 0, 1, 2, 3, 4),
+    (4, 3, 0, 5, 1, 2),
+    (5, 0, 3, 4, 2, 1),
+    (1, 2, 5, 0, 3, 4),
+    (4, 3, 1, 2, 0, 5),
 )
 GRAM_PAIRS = ((2, 3), (5, 0))
 PAIRS = tuple(sorted({tuple(sorted(links[i : i + 2])) for links in LINKS + GRAM_PAIRS for i in range(0, len(links), 2)}))
 ORDER = (
     ("products", 0), ("p", 0), ("products", 1), ("p", 1), ("p", 0), ("products", 2), ("p", 2), ("p", 1),
-    ("p", 2), ("p", 0), ("p", 0), ("terms", 0), ("p", 1), ("sum", 0), ("terms", 1), ("sum", 1), ("gram", 0),
-    ("p", 1), ("terms", 2), ("p", 2), ("sum", 2), ("sum", 0), ("sum", 1), ("terms", 3), ("sum", 3),
-    ("gram", 1), ("p", 2), ("terms", 4), ("sum", 4), ("sum", 2), ("terms", 5), ("sum", 5), ("sum", 3),
-    ("gram", 2), ("gram", 0), ("sum", 4), ("sum", 5), ("sum", 0), ("gram", 1), ("sum", 1), ("gram", 2),
-    ("sum", 2), ("sum", 5), ("sum", 4), ("sum", 3), ("sum", 0), ("sum", 1), ("gram", 0), ("gram", 1),
-    ("sum", 2), ("gram", 2), ("sum", 4), ("sum", 5), ("gram", 0), ("sum", 3), ("gram", 1), ("sum", 0),
-    ("gram", 2), ("sum", 1), ("gram", 0), ("sum", 2), ("gram", 1), ("gram", 2), ("factor", 1), ("factor", 1),
-    ("sum", 4), ("sum", 3), ("sum", 5), ("factor", 1), ("sum", 0), ("sum", 1), ("sum", 2), ("factor", 1),
-    ("factor", 1), ("factor", 1), ("sum", 4), ("factor", 1), ("sum", 3), ("sum", 5), ("factor", 1),
-    ("factor", 1), ("sum", 0), ("factor", 1), ("factor", 1), ("sum", 1), ("sum", 2), ("sum", 0),
-    ("factor", 1), ("factor", 1), ("sum", 1), ("factor", 1), ("sum", 4), ("sum", 5), ("sum", 2),
-    ("factor", 1), ("sum", 3), ("factor", 1), ("factor", 1), ("factor", 1), ("factor", 1), ("sum", 4),
-    ("sum", 5), ("sum", 3),
+    ("p", 2), ("p", 0), ("p", 0), ("terms", 0), ("sum", 0), ("terms", 1), ("p", 1), ("sum", 1), ("gram", 0),
+    ("sum", 0), ("p", 1), ("terms", 2), ("sum", 2), ("sum", 1), ("p", 2), ("terms", 3), ("sum", 3),
+    ("gram", 1), ("p", 2), ("sum", 2), ("terms", 4), ("sum", 4), ("sum", 3), ("terms", 5), ("sum", 5),
+    ("gram", 2), ("sum", 4), ("gram", 0), ("sum", 5), ("sum", 0), ("sum", 1), ("gram", 1), ("sum", 2),
+    ("gram", 2), ("sum", 4), ("sum", 3), ("sum", 1), ("gram", 0), ("sum", 5), ("sum", 2), ("sum", 0),
+    ("gram", 1), ("gram", 2), ("gram", 0), ("sum", 4), ("sum", 3), ("gram", 0), ("sum", 5), ("sum", 1),
+    ("sum", 2), ("gram", 1), ("gram", 2), ("sum", 0), ("gram", 1), ("gram", 2), ("factor", 1), ("factor", 1),
+    ("sum", 3), ("sum", 4), ("factor", 1), ("sum", 5), ("sum", 1), ("sum", 2), ("factor", 1), ("sum", 0),
+    ("factor", 1), ("factor", 1), ("factor", 1), ("sum", 3), ("sum", 4), ("sum", 5), ("factor", 1),
+    ("factor", 1), ("factor", 1), ("factor", 1), ("factor", 1), ("sum", 1), ("sum", 2), ("sum", 0),
+    ("factor", 1), ("factor", 1), ("sum", 1), ("sum", 2), ("factor", 1), ("sum", 0), ("factor", 1),
+    ("sum", 3), ("factor", 1), ("sum", 4), ("sum", 5), ("factor", 1), ("factor", 1), ("sum", 3), ("sum", 4),
+    ("sum", 5),
 )
 NT = (((1,), (1,)), ((), ()))
 
@@ -395,31 +395,23 @@
         copy.wait_send()
 
 
-def finish_kernel(g_sum, lhs_err, lhs_q, m_ref, err_hbm, q_out, ebuf, new_q, wst, store_sem, q_sem):
+def finish_kernel(g_sum, lhs_err, lhs_q, m_ref, err_hbm, q_out, ebuf, new_q, store_sem, q_sem):
     stores = []
     for m in range(MATS):
-        gh, gl = split(g_sum[m, :, :D] * 0.25)
-        wst[0, 0:64] = gh
-        wst[0, 64:128] = gh
-        wst[0, 128:192] = gl
-        fresh = dot(lhs_q[m, :, :192], wst[0])
-        new_q[m] = fresh
+        for i, (start, size) in enumerate(COLS):
+            cols, place = slice(start, start + size), pl.ds(start, size)
+            gh, gl = split(g_sum[m, :, cols] * 0.25)
+            fresh = dot(lhs_q[m, :, :192], jnp.concatenate([gh, gh, gl], axis=0))
+            new_q[m, :, cols] = fresh
+            nh, nl = split(fresh)
+            approx = dot(lhs_err[m, :, :192], jnp.concatenate([nh, nh, nl], axis=0))
+            ebuf[m, :, cols] = m_ref[m, :, cols] - approx
+            store = pltpu.make_async_copy(ebuf.at[m, :, place], err_hbm.at[0, m, :, place], store_sem.at[m, i])
+            store.start()
+            stores.append(store)
         store = pltpu.make_async_copy(new_q.at[m], q_out.at[m], q_sem.at[m])
         store.start()
         stores.append(store)
-        nh, nl = split(fresh)
-        wst[1, 0:64] = nh
-        wst[1, 64:128] = nh
-        wst[1, 128:192] = nl
-        for i, (start, size) in enumerate(COLS):
-            cols = slice(start, start + size)
-            ebuf[m, :, cols] = m_ref[m, :, cols] - dot(lhs_err[m, :, :192], wst[1, :, cols])
-            place = pl.ds(start, size)
-            store = pltpu.make_async_copy(
-                ebuf.at[m, :, place], err_hbm.at[0, m, :, place], store_sem.at[m, i]
-            )
-            store.start()
-            stores.append(store)
     for store in stores:
         store.wait()
 
@@ -487,7 +479,6 @@
         scratch_shapes=[
             pltpu.VMEM((MATS, ROWS, D), f32),
             pltpu.VMEM((MATS, R, D), f32),
-            pltpu.VMEM((2, ROWS, D), bf16),
             sem((MATS, 3)),
             sem((MATS,)),
         ],

time: 51.3 us -> 53.1 us (1.035)
  Pallas kernels: 50.6 us -> 52.3 us
    pallas_call x1, Pallas kernels: 3.92 us -> 5.01 us  [body(): pl.pallas_call(finish_kernel, out_shape=(jax.ShapeDtypeStruct((1, MATS, R...]
    pallas_call x1, Pallas kernels: 46.6 us -> 47.3 us  [body(): pl.pallas_call(comm_kernel, out_shape=(jax.ShapeDtypeStruct((MATS, R, 4 *...]
where the time goes in v12:
time: 53.1 us; the launch traced here: 53 us
  Pallas kernels  52.3 us (98%)
  between operations  0.64 us (1%)
    pallas_call x1, Pallas kernels, body(): pl.pallas_call(comm_kernel, out_shape=(jax.ShapeDtypeStruct((MATS, R, 4 *...  47.3 us
    pallas_call x1, Pallas kernels, body(): pl.pallas_call(finish_kernel, out_shape=(jax.ShapeDtypeStruct((1, MATS, R...  5.01 us

profile of v12, /device:TPU:1, one launch (start us, length us, event | category | flops | bytes accessed | tf_op | source)
XLA Modules:
  0.0 53.0 jit_solution(264673321542134378)
XLA Ops:
  0.6 47.3 %compress_and_sum.1 = (f32[6,64,1536]{2,1,0:T(8,128)S(1)}, bf16[6,192,256]{2,1,0:T(8,128)(2,1)S(1)}, bf16[6,64,256]{2,1,0:T(8,128)(2,1)S(1)}, f32[6,192,1408]{2,1,0:T(8,128)S(1)}) custom-call(bf16[1,6,192,1408]{3,2,1,0:T(8,128)(2,1)} %g_hbm.1, f32[1,6,192,1408]{3,2,1,0:T(8,128)} %e_hbm.1, f32[6,64,1408]{2,1,0:T(8,128)} %q_hbm.1), custom_call_target="tpu_custom_call" | custom-call | tf_op jit(solution)/shard_map/compress_and_sum/pallas_call | solution.py:423
  48.0 5.0 %new_q_and_errors.1 = (f32[1,6,192,1408]{3,2,1,0:T(8,128)}, f32[6,64,1408]{2,1,0:T(8,128)}) custom-call(f32[6,64,1536]{2,1,0:T(8,128)S(1)} %get-tuple-element.6.g_sum, bf16[6,192,256]{2,1,0:T(8,128)(2,1)S(1)} %get-tuple-element.7.lhs_err, bf16[6,64,256]{2,1,0:T(8,128)(2,1)S(1)} %get-tuple-element.8.lhs_q, f32[6,192,1408]{2,1,0:T(8,128)S(1)} %get-tuple-element.9.m_ref), custom_call_target="tpu_custom_call" | custom-call | tf_op jit(solution)/shard_map/new_q_and_errors/pallas_call | solution.py:471

commit v13 on v10

--- a/solution.py
+++ b/solution.py
@@ -320,14 +320,9 @@
 
         rows, other_rows = both_ways(tile, 0)
         own, others = both_ways(block, 2)
-        far_rows = pl.ds(pl.multiple_of(core * 32 + 16 - 16 * sides[link[0]], 16), 16)
 
         def send(s, src, dst, i):
             return three(src, dst, a_send.at[s, m], a_arrive.at[s, m], link[i], link[i + 1])
-
-        def forward(i, where):
-            part = g_sum.at[m, where, pl.ds(0, D)]
-            return remote(part, part, c_send.at[i, m], c_arrive.at[i, m], twin)
 
         def wait(copies):
             for copy in copies:
@@ -355,12 +350,12 @@
         wait(copies)
         whole = g_sum.at[m, rows, pl.ds(0, D)]
         copies = send(4, lambda f: whole, lambda f: whole, 0)
-        passed = [forward(1, rows)]
         yield
         wait(copies)
-        passed += [forward(2, other_rows[0]), forward(3, far_rows)]
-        yield
-        wait(passed)
+        half = g_sum.at[m, pl.ds(keep, 32), pl.ds(0, D)]
+        copy = remote(half, half, c_send.at[1, m], c_arrive.at[1, m], twin)
+        yield
+        copy.wait_recv()
 
     gc = [gram_chain(j) for j in range(3)]
     ac = [g_chain(m) for m in range(MATS)]
@@ -397,23 +392,29 @@
 
 def finish_kernel(g_sum, lhs_err, lhs_q, m_ref, err_hbm, q_out, ebuf, new_q, wst, store_sem, q_sem):
     stores = []
-    for m in range(MATS):
+
+    def fresh(m):
         gh, gl = split(g_sum[m, :, :D] * 0.25)
-        wst[0, 0:64] = gh
-        wst[0, 64:128] = gh
-        wst[0, 128:192] = gl
-        fresh = dot(lhs_q[m, :, :192], wst[0])
-        new_q[m] = fresh
+        wst[m % 2, 0, 0:64] = gh
+        wst[m % 2, 0, 64:128] = gh
+        wst[m % 2, 0, 128:192] = gl
+        value = dot(lhs_q[m, :, :192], wst[m % 2, 0])
+        new_q[m] = value
         store = pltpu.make_async_copy(new_q.at[m], q_out.at[m], q_sem.at[m])
         store.start()
         stores.append(store)
-        nh, nl = split(fresh)
-        wst[1, 0:64] = nh
-        wst[1, 64:128] = nh
-        wst[1, 128:192] = nl
+        nh, nl = split(value)
+        wst[m % 2, 1, 0:64] = nh
+        wst[m % 2, 1, 64:128] = nh
+        wst[m % 2, 1, 128:192] = nl
+
+    fresh(0)
+    for m in range(MATS):
+        if m + 1 < MATS:
+            fresh(m + 1)
         for i, (start, size) in enumerate(COLS):
             cols = slice(start, start + size)
-            ebuf[m, :, cols] = m_ref[m, :, cols] - dot(lhs_err[m, :, :192], wst[1, :, cols])
+            ebuf[m, :, cols] = m_ref[m, :, cols] - dot(lhs_err[m, :, :192], wst[m % 2, 1, :, cols])
             place = pl.ds(start, size)
             store = pltpu.make_async_copy(
                 ebuf.at[m, :, place], err_hbm.at[0, m, :, place], store_sem.at[m, i]
@@ -464,8 +465,8 @@
             sem((MATS, 3)),
             sem((3, 3)),
             sem((3, 3)),
-            sem((4, MATS)),
-            sem((4, MATS)),
+            sem((2, MATS)),
+            sem((2, MATS)),
             sem((5, MATS, 3)),
             sem((5, MATS, 3)),
             sem((3, 3, 3)),
@@ -487,7 +488,7 @@
         scratch_shapes=[
             pltpu.VMEM((MATS, ROWS, D), f32),
             pltpu.VMEM((MATS, R, D), f32),
-            pltpu.VMEM((2, ROWS, D), bf16),
+            pltpu.VMEM((2, 2, ROWS, D), bf16),
             sem((MATS, 3)),
             sem((MATS,)),
         ],

time: 51.3 us -> 51.3 us (level)
  no operation moved by 1% of the time
where the time goes in v13:
time: 51.3 us; the launch traced here: 51.2 us
  Pallas kernels  50.6 us (99%)
  between operations  0.64 us (1%)
    pallas_call x1, Pallas kernels, body(): pl.pallas_call(comm_kernel, out_shape=(jax.ShapeDtypeStruct((MATS, R, 4 *...  46.5 us
    pallas_call x1, Pallas kernels, body(): pl.pallas_call(finish_kernel, out_shape=(jax.ShapeDtypeStruct((1, MATS, R...  4.03 us

profile of v13, /device:TPU:1, one launch (start us, length us, event | category | flops | bytes accessed | tf_op | source)
XLA Modules:
  0.0 51.2 jit_solution(289393481980502048)
XLA Ops:
  0.6 46.5 %compress_and_sum.1 = (f32[6,64,1536]{2,1,0:T(8,128)S(1)}, bf16[6,192,256]{2,1,0:T(8,128)(2,1)S(1)}, bf16[6,64,256]{2,1,0:T(8,128)(2,1)S(1)}, f32[6,192,1408]{2,1,0:T(8,128)S(1)}) custom-call(bf16[1,6,192,1408]{3,2,1,0:T(8,128)(2,1)} %g_hbm.1, f32[1,6,192,1408]{3,2,1,0:T(8,128)} %e_hbm.1, f32[6,64,1408]{2,1,0:T(8,128)} %q_hbm.1), custom_call_target="tpu_custom_call" | custom-call | tf_op jit(solution)/shard_map/compress_and_sum/pallas_call | solution.py:432
  47.2 4.0 %new_q_and_errors.1 = (f32[1,6,192,1408]{3,2,1,0:T(8,128)}, f32[6,64,1408]{2,1,0:T(8,128)}) custom-call(f32[6,64,1536]{2,1,0:T(8,128)S(1)} %get-tuple-element.6.g_sum, bf16[6,192,256]{2,1,0:T(8,128)(2,1)S(1)} %get-tuple-element.7.lhs_err, bf16[6,64,256]{2,1,0:T(8,128)(2,1)S(1)} %get-tuple-element.8.lhs_q, f32[6,192,1408]{2,1,0:T(8,128)S(1)} %get-tuple-element.9.m_ref), custom_call_target="tpu_custom_call" | custom-call | tf_op jit(solution)/shard_map/new_q_and_errors/pallas_call | solution.py:480

commit v14 on v10

--- a/solution.py
+++ b/solution.py
@@ -11,6 +11,7 @@
 MATS, ROWS, D, R = 6, 192, 1408, 64
 HALF = ROWS // 2
 BLOCK = 384
+LAG = 16
 COLS = ((0, 512), (512, 512), (1024, 384))
 f32, bf16 = jnp.float32, jnp.bfloat16
 LINKS = (
@@ -184,6 +185,7 @@
         pl.semaphore_signal(barrier, inc=1, device_id=other, device_id_type=MESH)
 
     sent = []
+    step = 0
 
     def remote(src, dst, send, arrive, target):
         copy = pltpu.make_async_remote_copy(
@@ -191,7 +193,7 @@
             device_id=target, device_id_type=MESH,
         )
         copy.start()
-        sent.append(copy)
+        sent.append((step, copy))
         return copy
 
     mine = pl.multiple_of(core * HALF, 8)
@@ -320,14 +322,9 @@
 
         rows, other_rows = both_ways(tile, 0)
         own, others = both_ways(block, 2)
-        far_rows = pl.ds(pl.multiple_of(core * 32 + 16 - 16 * sides[link[0]], 16), 16)
 
         def send(s, src, dst, i):
             return three(src, dst, a_send.at[s, m], a_arrive.at[s, m], link[i], link[i + 1])
-
-        def forward(i, where):
-            part = g_sum.at[m, where, pl.ds(0, D)]
-            return remote(part, part, c_send.at[i, m], c_arrive.at[i, m], twin)
 
         def wait(copies):
             for copy in copies:
@@ -355,19 +352,21 @@
         wait(copies)
         whole = g_sum.at[m, rows, pl.ds(0, D)]
         copies = send(4, lambda f: whole, lambda f: whole, 0)
-        passed = [forward(1, rows)]
         yield
         wait(copies)
-        passed += [forward(2, other_rows[0]), forward(3, far_rows)]
-        yield
-        wait(passed)
+        half = g_sum.at[m, pl.ds(keep, 32), pl.ds(0, D)]
+        copy = remote(half, half, c_send.at[1, m], c_arrive.at[1, m], twin)
+        yield
+        copy.wait_recv()
 
     gc = [gram_chain(j) for j in range(3)]
     ac = [g_chain(m) for m in range(MATS)]
     factor = None
 
     p_stage = [0, 0, 0]
-    for what, i in ORDER:
+    for step, (what, i) in enumerate(ORDER):
+        while sent and sent[0][0] <= step - LAG:
+            sent.pop(0)[1].wait_send()
         if what == "products":
             local_p(i)
             if i == 0:
@@ -375,6 +374,9 @@
         elif what == "p":
             p_step(p_stage[i], i)
             p_stage[i] += 1
+            if p_stage[i] == 4:
+                for k in range(3):
+                    p_copy(k, i).wait_send()
         elif what == "gram":
             next(gc[i], None)
         elif what == "terms":
@@ -388,10 +390,7 @@
                 next(factor, None)
     for _ in factor:
         pass
-    for s in range(3):
-        for j in range(3):
-            p_copy(s, j).wait_send()
-    for copy in sent:
+    for _, copy in sent:
         copy.wait_send()
 
 
@@ -464,8 +463,8 @@
             sem((MATS, 3)),
             sem((3, 3)),
             sem((3, 3)),
-            sem((4, MATS)),
-            sem((4, MATS)),
+            sem((2, MATS)),
+            sem((2, MATS)),
             sem((5, MATS, 3)),
             sem((5, MATS, 3)),
             sem((3, 3, 3)),

time: 51.3 us -> 51 us (level)
  no operation moved by 1% of the time
where the time goes in v14:
time: 51 us; the launch traced here: 50.9 us
  Pallas kernels  50.3 us (99%)
  between operations  0.64 us (1%)
    pallas_call x1, Pallas kernels, body(): pl.pallas_call(comm_kernel, out_shape=(jax.ShapeDtypeStruct((MATS, R, 4 *...  46.4 us
    pallas_call x1, Pallas kernels, body(): pl.pallas_call(finish_kernel, out_shape=(jax.ShapeDtypeStruct((1, MATS, R...  3.92 us

profile of v14, /device:TPU:1, one launch (start us, length us, event | category | flops | bytes accessed | tf_op | source)
XLA Modules:
  0.0 50.9 jit_solution(16814292132633330415)
XLA Ops:
  0.6 46.4 %compress_and_sum.1 = (f32[6,64,1536]{2,1,0:T(8,128)S(1)}, bf16[6,192,256]{2,1,0:T(8,128)(2,1)S(1)}, bf16[6,64,256]{2,1,0:T(8,128)(2,1)S(1)}, f32[6,192,1408]{2,1,0:T(8,128)S(1)}) custom-call(bf16[1,6,192,1408]{3,2,1,0:T(8,128)(2,1)} %g_hbm.1, f32[1,6,192,1408]{3,2,1,0:T(8,128)} %e_hbm.1, f32[6,64,1408]{2,1,0:T(8,128)} %q_hbm.1), custom_call_target="tpu_custom_call" | custom-call | tf_op jit(solution)/shard_map/compress_and_sum/pallas_call | solution.py:430
  47.0 3.9 %new_q_and_errors.1 = (f32[1,6,192,1408]{3,2,1,0:T(8,128)}, f32[6,64,1408]{2,1,0:T(8,128)}) custom-call(f32[6,64,1536]{2,1,0:T(8,128)S(1)} %get-tuple-element.6.g_sum, bf16[6,192,256]{2,1,0:T(8,128)(2,1)S(1)} %get-tuple-element.7.lhs_err, bf16[6,64,256]{2,1,0:T(8,128)(2,1)S(1)} %get-tuple-element.8.lhs_q, f32[6,192,1408]{2,1,0:T(8,128)S(1)} %get-tuple-element.9.m_ref), custom_call_target="tpu_custom_call" | custom-call | tf_op jit(solution)/shard_map/new_q_and_errors/pallas_call | solution.py:478

commit v15 on v14

--- a/solution.py
+++ b/solution.py
@@ -198,7 +198,6 @@
 
     mine = pl.multiple_of(core * HALF, 8)
     theirs = pl.multiple_of((1 - core) * HALF, 8)
-    qst[...] = jnp.zeros_like(qst)
     q_acc[...] = jnp.zeros_like(q_acc)
 
     def arrive(m):
@@ -215,23 +214,25 @@
             ml[m, rows] = lo
         b = m % 2
         hi, lo = split(qbuf[m])
-        qst[b, 64 * b : 64 * b + 64] = hi
-        qst[b, 128 + 64 * b : 192 + 64 * b] = lo
+        qst[b, 0:64] = hi
+        qst[b, 64:128] = lo
+        qst[b, 128:192] = hi
+        qst[b, 192:256] = hi
 
     def local_p(j):
         if j == 0:
             arrive(0)
             merge(0)
-        total = None
+        parts = []
         for m in (2 * j, 2 * j + 1):
             if m + 1 < MATS:
                 arrive(m + 1)
-            wide = dot_nt(mh[m], qst[m % 2])
-            part = wide[:, :128] + wide[:, 128:] + dot_nt(ml[m], qst[m % 2, :128])
+            wide = dot_nt(mh[m], qst[m % 2, :128])
+            parts.append(wide + pltpu.roll(wide, 64, axis=1) + dot_nt(ml[m], qst[m % 2, 128:]))
             if m + 1 < MATS:
                 merge(m + 1)
-            total = part if total is None else total + part
-        p_own[j] = total
+        lane = lax.broadcasted_iota(jnp.int32, (ROWS, 2 * R), 1)
+        p_own[j] = jnp.where(lane < 64, parts[0], parts[1])
 
     def p_copy(s, j):
         if s == 0:

time: 51 us -> 50.6 us (level)
  no operation moved by 1% of the time
where the time goes in v15:
time: 50.6 us; the launch traced here: 50.5 us
  Pallas kernels  49.9 us (99%)
  between operations  0.64 us (1%)
    pallas_call x1, Pallas kernels, body(): pl.pallas_call(comm_kernel, out_shape=(jax.ShapeDtypeStruct((MATS, R, 4 *...  46 us
    pallas_call x1, Pallas kernels, body(): pl.pallas_call(finish_kernel, out_shape=(jax.ShapeDtypeStruct((1, MATS, R...  3.92 us

profile of v15, /device:TPU:1, one launch (start us, length us, event | category | flops | bytes accessed | tf_op | source)
XLA Modules:
  0.0 50.5 jit_solution(17280197083419140598)
XLA Ops:
  0.6 46.0 %compress_and_sum.1 = (f32[6,64,1536]{2,1,0:T(8,128)S(1)}, bf16[6,192,256]{2,1,0:T(8,128)(2,1)S(1)}, bf16[6,64,256]{2,1,0:T(8,128)(2,1)S(1)}, f32[6,192,1408]{2,1,0:T(8,128)S(1)}) custom-call(bf16[1,6,192,1408]{3,2,1,0:T(8,128)(2,1)} %g_hbm.1, f32[1,6,192,1408]{3,2,1,0:T(8,128)} %e_hbm.1, f32[6,64,1408]{2,1,0:T(8,128)} %q_hbm.1), custom_call_target="tpu_custom_call" | custom-call | tf_op jit(solution)/shard_map/compress_and_sum/pallas_call | solution.py:431
  46.6 3.9 %new_q_and_errors.1 = (f32[1,6,192,1408]{3,2,1,0:T(8,128)}, f32[6,64,1408]{2,1,0:T(8,128)}) custom-call(f32[6,64,1536]{2,1,0:T(8,128)S(1)} %get-tuple-element.6.g_sum, bf16[6,192,256]{2,1,0:T(8,128)(2,1)S(1)} %get-tuple-element.7.lhs_err, bf16[6,64,256]{2,1,0:T(8,128)(2,1)S(1)} %get-tuple-element.8.lhs_q, f32[6,192,1408]{2,1,0:T(8,128)S(1)} %get-tuple-element.9.m_ref), custom_call_target="tpu_custom_call" | custom-call | tf_op jit(solution)/shard_map/new_q_and_errors/pallas_call | solution.py:479
